TPU v7x, 512 devices: a whole 4x4x16 slice. The times are simulated.
512 devices in a mesh: aux: 64 (over x, z), ao: 8 (over y, core).
Axes of the slice: x: 4, y: 4, z: 16, core: 2. Of those that a mesh axis runs over, the one named last changes fastest.
Arguments:
- pair_integrals: bfloat16 [64, 192, 128, 128], P('aux', 'ao'), may hold values from -6 to 6
- occ_coef: bfloat16 [320, 6144], replicated, may hold values from -0.5 to 0.5
- vir_coef: bfloat16 [6144, 5760], P('aux', 'ao'), may hold values from -0.078125 to 0.078125
- metric_factor: bfloat16 [64, 64], replicated, may hold values from -0.75 to 0.75
- block_rows: int32 [192], replicated, may hold values from 0 to 47, as said below
- block_cols: int32 [192], replicated, may hold values from 0 to 47, as said below
- block_count: int32 [8], replicated, may hold values from 6 to 24, as said below
- occ_order: int32 [320], replicated, may hold values from 0 to 319, each once
Outputs:
- factor_b: bfloat16 [64, 320, 5760], P(None, 'aux', 'ao')
Inputs may be any that keep to these rules, and one draw needn't show every extreme that they name: `block_rows`: slots of row group g name row blocks g * 6 to (g + 1) * 6 - 1; within a group no (row, column) pair repeats. `block_cols`: column blocks of any row group, in any order. `block_count`: exactly one row group fills all 24 slots in every draw.
All inputs are finite; a program needn't handle non-finite values.
Results may differ from a plain program's by a relative error of at most 0.017.
Values may be sent and summed in bfloat16 or wider, within the bound.
No kernel may reach another device: no remote copies, remote signals or barrier semaphores. Data moves between devices by JAX's collectives and lax.ppermute only.
A program may use at most 128 MiB of HBM per device.

v0:
```python
import jax
import jax.numpy as jnp
from jax import lax
from jax.sharding import PartitionSpec as P


def group_partial(blocks, occ_coef, block_rows, block_cols, count, base):
    width = blocks.shape[-1]

    def step(slot, total):
        index = base + slot
        row = block_rows[index]
        col = block_cols[index]
        coef = lax.dynamic_slice_in_dim(occ_coef, row * width, width, 1)
        block = lax.dynamic_index_in_dim(blocks, slot, 1, keepdims=False)
        term = jnp.einsum("im,pmn->pin", coef, block, preferred_element_type=jnp.float32)
        old = lax.dynamic_slice_in_dim(total, col * width, width, 2)
        return lax.dynamic_update_slice_in_dim(total, old + term, col * width, 2)

    start = jnp.zeros((blocks.shape[0], occ_coef.shape[0], occ_coef.shape[1]), jnp.float32)
    return lax.fori_loop(jnp.int32(0), count, step, start)


def shards(
    pair_integrals,
    occ_coef,
    vir_coef,
    metric_factor,
    block_rows,
    block_cols,
    block_count,
    occ_order,
):
    slab_aux = pair_integrals.shape[0]
    slot_total = pair_integrals.shape[1]
    occ_width, ao_width = occ_coef.shape
    group = lax.axis_index("ao")
    part = group_partial(
        pair_integrals, occ_coef, block_rows, block_cols, block_count[group], group * slot_total
    )
    share = lax.psum_scatter(part.astype(jnp.bfloat16), "ao", scatter_dimension=2, tiled=True)
    half = lax.all_gather(share, "ao", axis=2, tiled=True)
    coef_rows = lax.all_gather(vir_coef, "aux", axis=0, tiled=True)
    pencil = jnp.dot(
        half.reshape(slab_aux * occ_width, ao_width), coef_rows, preferred_element_type=jnp.float32
    )
    pencil = pencil.astype(jnp.bfloat16).reshape(slab_aux, occ_width, coef_rows.shape[1])
    chosen = jnp.take(pencil, occ_order, axis=1)
    owners = lax.axis_size("aux")
    chosen = chosen.reshape(slab_aux, owners, occ_width // owners, coef_rows.shape[1])
    mixed = jnp.einsum(
        "qp,pokv->qokv",
        metric_factor,
        lax.all_to_all(chosen, "aux", split_axis=1, concat_axis=0, tiled=True),
        preferred_element_type=jnp.float32,
    )
    result = mixed.astype(jnp.bfloat16)
    return result.reshape(result.shape[0], occ_width // owners, coef_rows.shape[1])


def solution(mesh):
    return jax.shard_map(
        shards,
        mesh=mesh,
        in_specs=(P("aux", "ao", None, None), P(), P("aux", "ao"), P(), P(), P(), P(), P()),
        out_specs=P(None, "aux", "ao"),
        check_vma=False,
    )
```

profile of v0, /device:TPU:54, one launch (start us, length us, event | category | flops | bytes accessed | tf_op | source)
XLA Modules:
  0.0 448.5 jit_solution(970365218422497641)
XLA Ops:
  6.6 1.3 dynamic_slice.19
  7.9 4.0 broadcast_in_dim.19
  11.9 59.5 %while.10 = (s32[]{:T(128)}, f32[1,320,6144]{2,1,0:T(8,128)}, s32[]{:T(128)}, s32[]{:T(128)}, s32[192]{0:T(256)S(1)}, /*index=5*/bf16[1,24,128,128]{3,2,1,0:T(8,...) while((s32[]{:T(128)}, f32[1,320,6144]{2,1,0:T(8,128)}, ...), condition=%wide.region_1.2_spmd, body=%wide.region_0.1_spmd.sunk | while | flops 10526737 | bytes 442709 | solution.py:21
  14.9 1.9 fusion.21
  19.9 1.8 fusion.21
  24.7 1.8 fusion.21
  29.6 1.8 fusion.21
  34.5 1.8 fusion.21
  39.4 1.8 fusion.21
  44.3 1.8 fusion.21
  49.2 1.8 fusion.21
  54.1 1.8 fusion.21
  59.0 1.8 fusion.21
  63.9 1.9 fusion.21
  68.8 1.9 fusion.21
  71.4 5.8 %convert_element_type.13 = bf16[1,320,6144]{2,1,0:T(8,128)(2,1)} convert(f32[1,320,6144]{2,1,0:T(8,128)} %get-tuple-element.48) | non-fusion elementwise | flops 1966080 | bytes 11796480 | tf_op jit(solution)/shard_map/convert_element_type | solution.py:41
  77.2 100.4 %reduce-scatter.2.cloned.1.call-done = bf16[1,320,768]{2,1,0:T(8,128)(2,1)} async-done(((bf16[1,320,6144]{2,1,0:T(8,128)(2,1)}), bf16[1,320,768]{2,1,0:T(8,128)(2,1)}) %reduce-scatter.2.cloned.1.call-update) | async-done | bytes 491536 | tf_op jit(solution)/shard_map/reduce_scatter | solution.py:41
  177.7 0.7 all-gather.5.cloned.1.call-update
  178.6 42.3 %all-gather.3.cloned.1.call-done = bf16[1,320,6144]{2,1,0:T(8,128)(2,1)} async-done(((bf16[1,320,768]{2,1,0:T(8,128)(2,1)}), bf16[1,320,6144]{2,1,0:T(8,128)(2,1)}) %all-gather.3.cloned.1.call-update) | async-done | bytes 3932176 | tf_op jit(solution)/shard_map/all_gather | solution.py:42
  220.9 162.7 %all-gather.5.cloned.1.call-done = bf16[6144,720]{1,0:T(8,128)(2,1)} async-done(((bf16[96,720]{1,0:T(8,128)(2,1)}), bf16[6144,720]{1,0:T(8,128)(2,1)}) %all-gather.5.cloned.1.call-update) | async-done | bytes 8847376 | tf_op jit(solution)/shard_map/all_gather | solution.py:43
  383.6 8.1 %fusion.8 = bf16[320,720]{1,0:T(8,128)(2,1)S(1)} fusion(bf16[6144,720]{1,0:T(8,128)(2,1)} %all-gather.5.cloned.1.call-done, bf16[1,320,6144]{2,1,0:T(8,128)(2,1)} %all-gather.3.cloned.1.call-done), kind=kOutput, calls=%fused_computation.10 | convolution fusion | flops 2831385600 | bytes 13240320 | tf_op jit(solution)/shard_map/dot_general | solution.py:44
  391.6 2.1 gather_fusion
  394.2 46.7 %all_to_all.4 = bf16[1,64,5,720]{3,2,0,1:T(8,128)(2,1)S(1)} all-to-all(bf16[1,64,5,720]{3,2,0,1:T(8,128)(2,1)S(1)} %select_bitcast_fusion), channel_id=1, replica_groups=mesh['aux'=64,'ao'=8] {'aux'}, dimensions={1} | all-to-all | bytes 921600 | tf_op jit(solution)/shard_map/all_to_all | solution.py:54
  440.9 1.1 fusion.11
  (43 shorter events, 14.9 us)
Async XLA Ops:
  6.5 434.3 %copy-start = (bf16[64,64]{1,0:T(8,128)(2,1)S(1)}, bf16[64,64]{1,0:T(8,128)(2,1)}, u32[]{:S(2)}) copy-start(bf16[64,64]{1,0:T(8,128)(2,1)} %param.13) | copy-start | bytes 24580
  6.5 5.3 %copy-start.3 = (s32[192]{0:T(256)S(1)}, s32[192]{0:T(256)}, u32[]{:S(2)}) copy-start(s32[192]{0:T(256)} %param.14) | copy-start | bytes 2308
  6.5 5.3 %copy-start.2 = (s32[192]{0:T(256)S(1)}, s32[192]{0:T(256)}, u32[]{:S(2)}) copy-start(s32[192]{0:T(256)} %param.15) | copy-start | bytes 2308
  6.5 171.1 %reduce-scatter.2.cloned.1.call-start = ((), (), s32[]{:S(2)}) async-start(), calls=%async_computation.2 | async-start | bytes 4423680 | tf_op jit(solution)/shard_map/reduce_scatter | solution.py:41
  71.4 107.0 %copy-start.1 = (s32[320]{0:T(512)S(1)}, s32[320]{0:T(512)}, u32[]{:S(2)}) copy-start(s32[320]{0:T(512)} %param.17) | copy-start | bytes 3844
  77.2 143.7 %all-gather.3.cloned.1.call-start = ((), (), s32[]{:S(2)}) async-start(), calls=%async_computation.3 | async-start | bytes 4423680 | tf_op jit(solution)/shard_map/all_gather | solution.py:42
  177.6 205.9 %all-gather.5.cloned.1.call-start = ((), (), s32[]{:S(2)}) async-start(), calls=%async_computation.4 | async-start | bytes 9584640 | tf_op jit(solution)/shard_map/all_gather | solution.py:43
Sparse Core Ops, SparseCore 0:
  77.3 100.2 reduce-scatter.1
  179.7 41.0 all-gather.2
  223.8 159.6 all-gather.4
where the time goes:
time: 451 us; the launch traced here: 448 us
  waiting for transfers between devices  306 us (68%)
  blocking collectives  46.7 us (10%)
  matrix products  31.3 us (7%)
  loops' own time  23.1 us (5%)
  local copies, waits for them, and re-layouts  22 us (5%)
  between operations  13.2 us (3%)
  other arithmetic  5.93 us (1%)
    all_gather x1, waiting for transfers between devices, shards(): coef_rows = lax.all_gather(vir_coef, 'aux', axis=0, tiled=True)  163 us
    reduce_scatter x1, waiting for transfers between devices, shards(): lax.psum_scatter(part.astype(jnp.bfloat16), 'ao', scatter_dimension=2, ti...  100 us
    all_to_all x1, blocking collectives, shards(): lax.all_to_all(chosen, 'aux', split_axis=1, concat_axis=0, tiled=True)  46.7 us
    all_gather x1, waiting for transfers between devices, shards(): half = lax.all_gather(share, 'ao', axis=2, tiled=True)  42.3 us
    another operation x1, loops' own time, group_partial(): return lax.fori_loop(jnp.int32(0), count, step, start)  23.1 us
    dot_general x12, matrix products, step(): jnp.einsum('im,pmn->pin', coef, block, preferred_element_type=jnp.float32)  22.2 us
  transfers between devices with their start and end apart: 3, of which 3 were waited for; matrix products, arithmetic and copies ran while one was open for 0% of the time, Pallas kernels for 0%

commit v1 on v0

v1 whole, which is shorter than its diff:
```python
import jax
import jax.numpy as jnp
from jax import lax
from jax.experimental import pallas as pl
from jax.experimental.pallas import tpu as pltpu
from jax.sharding import Mesh, PartitionSpec as P

GROUP_ROWS = 6


def partial_kernel(
    rows, cols, counts, place, own, other, occ, order, out, total, coef, *, slots, width, blocks_x
):
    y, core = place[0], place[1]
    occ_width = occ.shape[0]
    half_blocks = blocks_x // 2
    pick = lax.broadcasted_iota(jnp.int32, (occ_width, occ_width), 1) == order[...]
    pick = jnp.where(pick, 1.0, 0.0).astype(jnp.bfloat16)
    for row in range(coef.shape[0]):
        chosen = jnp.dot(
            pick, occ[:, row * width : (row + 1) * width], preferred_element_type=jnp.float32
        )
        coef[row] = chosen.astype(jnp.bfloat16)
    total[...] = jnp.zeros_like(total)

    for which, blocks in ((core, own), (1 - core, other)):
        group = 2 * y + which

        @pl.loop(0, counts[group])
        def _(slot):
            col = cols[group * slots + slot]
            inside = lax.rem(col, blocks_x)

            @pl.when(inside // half_blocks == core)
            def _():
                row = rows[group * slots + slot] - 2 * y * GROUP_ROWS
                local = (col // blocks_x) * half_blocks + lax.rem(inside, half_blocks)
                total[local] += jnp.dot(
                    coef[row], blocks[slot], preferred_element_type=jnp.float32
                )

    for block in range(total.shape[0]):
        out[:, block * width : (block + 1) * width] = total[block].astype(out.dtype)


def group_partial(own, other, occ_coef, order, rows, cols, counts, place, blocks_x):
    slots, width = own.shape[0], own.shape[1]
    occ_width, ao_width = occ_coef.shape
    half_blocks = ao_width // width // 2
    kernel = lambda *refs: partial_kernel(*refs, slots=slots, width=width, blocks_x=blocks_x)
    whole = lambda *shape: pl.BlockSpec(shape, lambda i, *_: (0,) * len(shape))
    return pl.pallas_call(
        kernel,
        grid_spec=pltpu.PrefetchScalarGridSpec(
            num_scalar_prefetch=4,
            grid=(1,),
            in_specs=[
                whole(slots, width, width),
                whole(slots, width, width),
                pl.BlockSpec(
                    (occ_width, 2 * GROUP_ROWS * width), lambda i, r, c, n, place: (0, place[0])
                ),
                whole(occ_width, 1),
            ],
            out_specs=whole(occ_width, half_blocks * width),
            scratch_shapes=[
                pltpu.VMEM((half_blocks, occ_width, width), jnp.float32),
                pltpu.VMEM((2 * GROUP_ROWS, occ_width, width), jnp.bfloat16),
            ],
        ),
        out_shape=jax.ShapeDtypeStruct((occ_width, half_blocks * width), jnp.bfloat16),
        compiler_params=pltpu.CompilerParams(vmem_limit_bytes=40 << 20),
        name="group_partial",
    )(rows, cols, counts, place, own, other, occ_coef, order)


def shift(value, axis, step):
    n = lax.axis_size(axis)
    return lax.ppermute(value, axis, [(i, (i + step) % n) for i in range(n)])


def add(*terms):
    total = terms[0].astype(jnp.float32)
    for term in terms[1:]:
        total = total + term.astype(jnp.float32)
    return total.astype(jnp.bfloat16)


def scatter_sum(chunk, axis):
    far = chunk(2)
    cut = far.shape[0] // 2
    from_left = shift(far[:cut], axis, 1)
    from_right = shift(far[cut:], axis, -1)
    right, left = chunk(1), chunk(3)
    right = jnp.concatenate([add(right[:cut], from_left), right[cut:]], 0)
    left = jnp.concatenate([left[:cut], add(left[cut:], from_right)], 0)
    return add(chunk(0), shift(right, axis, 1), shift(left, axis, -1))


def gather_ring(mine, axis):
    left = shift(mine, axis, 1)
    right = shift(mine, axis, -1)
    cut = mine.shape[0] // 2
    far = jnp.concatenate([shift(left[:cut], axis, 1), shift(right[cut:], axis, -1)], 0)
    return mine, right, far, left


def shards(
    pair_integrals,
    occ_coef,
    vir_coef,
    metric_factor,
    block_rows,
    block_cols,
    block_count,
    occ_order,
):
    x, y, core = lax.axis_index("x"), lax.axis_index("y"), lax.axis_index("c")
    nx, nz, ny = lax.axis_size("x"), lax.axis_size("z"), lax.axis_size("y")
    width = pair_integrals.shape[2]
    occ_width, ao_width = occ_coef.shape
    vir_width = vir_coef.shape[1]
    naux = nx * nz
    each = occ_width // naux
    blocks_x = ao_width // width // nx
    half_blocks = blocks_x // 2

    vir_rows = lax.all_gather(vir_coef, "z", axis=0, tiled=True)
    deep = vir_rows.shape[0] // 2
    vir_rows = jnp.concatenate(
        [
            lax.dynamic_slice_in_dim(vir_rows, core * deep, deep, 0),
            lax.dynamic_slice_in_dim(vir_rows, (1 - core) * deep, deep, 0),
        ],
        0,
    )

    own = pair_integrals[0]
    other = shift(own, "c", 1)
    order = occ_order.reshape(nx, nz, each).transpose(0, 2, 1).reshape(occ_width, 1)
    place = jnp.stack([y, core]).astype(jnp.int32)
    part = group_partial(
        own, other, occ_coef, order, block_rows, block_cols, block_count, place, blocks_x
    )
    part = part.reshape(ny, occ_width // ny, part.shape[1])
    share = scatter_sum(
        lambda d: lax.dynamic_index_in_dim(part, lax.rem(y + d, ny), 0, keepdims=False), "y"
    )
    send = share.reshape(each, nz, nx, half_blocks, width).transpose(2, 1, 0, 3, 4)
    send = send.reshape(naux, each * half_blocks, width)
    got = lax.all_to_all(send, ("x", "z"), 0, 0, tiled=True)
    mine = got.reshape(naux, each, half_blocks, width).transpose(1, 0, 2, 3)
    mine = mine.reshape(each * naux, half_blocks * width)
    pieces = jnp.stack(gather_ring(mine, "y"))
    pieces = jnp.concatenate([pieces, shift(pieces, "c", 1)], 2)

    def product(d):
        rows = lax.dynamic_index_in_dim(
            pieces, lax.rem(x + d - y + ny, ny), 0, keepdims=False
        )
        return jnp.dot(rows, vir_rows, preferred_element_type=jnp.float32).astype(jnp.bfloat16)

    pencil = scatter_sum(product, "x").reshape(each, naux, vir_width)
    mixed = jnp.einsum(
        "qp,kpv->qkv", metric_factor, pencil, preferred_element_type=jnp.float32
    )
    return mixed.astype(jnp.bfloat16)


def solution(mesh):
    aux, ao = mesh.devices.shape
    grid = Mesh(mesh.devices.reshape(4, aux // 4, ao // 2, 2), ("x", "z", "y", "c"))
    every = P()
    return jax.shard_map(
        shards,
        mesh=grid,
        in_specs=(P(("x", "z"), ("y", "c")), every, P(("x", "z"), ("y", "c"))) + (every,) * 5,
        out_specs=P(None, ("x", "z"), ("y", "c")),
        check_vma=False,
    )
```

time: 451 us -> 197 us (0.44)
  the two profiles are of different devices: /device:TPU:54 before, /device:TPU:22 now
where the time goes in v1:
time: 197 us; the launch traced here: 196 us
  waiting for transfers between devices  93.6 us (48%)
  starting transfers between devices  58.4 us (30%)
  between operations  13.8 us (7%)
  local copies, waits for them, and re-layouts  11.4 us (6%)
  other arithmetic  7.7 us (4%)
  matrix products  6.25 us (3%)
  Pallas kernels  4.49 us (2%)
    ppermute x14, waiting for transfers between devices, shift(): return lax.ppermute(value, axis, [(i, (i + step) % n) for i in range(n)])  43.8 us
    ppermute x14, starting transfers between devices, shift(): return lax.ppermute(value, axis, [(i, (i + step) % n) for i in range(n)])  39.5 us
    all_to_all x1, waiting for transfers between devices, shards(): got = lax.all_to_all(send, ('x', 'z'), 0, 0, tiled=True)  28.3 us
    all_gather x1, waiting for transfers between devices, shards(): vir_rows = lax.all_gather(vir_coef, 'z', axis=0, tiled=True)  20.8 us
    all_to_all x1, starting transfers between devices, shards(): got = lax.all_to_all(send, ('x', 'z'), 0, 0, tiled=True)  18.8 us
    unnamed x19, local copies, waits for them, and re-layouts  5.34 us
    dot_general x4, matrix products, product(): jnp.dot(rows, vir_rows, preferred_element_type=jnp.float32)  5.19 us
    pallas_call x1, Pallas kernels, group_partial(): pl.pallas_call(kernel, grid_spec=pltpu.PrefetchScalarGridSpec(num_scalar_...  4.49 us
  transfers between devices with their start and end apart: 16, of which 13 were waited for; matrix products, arithmetic and copies ran while one was open for 5% of the time, Pallas kernels for 0%

profile of v1, /device:TPU:22, one launch (start us, length us, event | category | flops | bytes accessed | tf_op | source)
XLA Modules:
  0.0 195.6 jit_solution(17706274018368835837)
XLA Ops:
  11.1 2.1 %copy-done.1 = bf16[320,6144]{1,0:T(8,128)(2,1)S(1)} copy-done((bf16[320,6144]{1,0:T(8,128)(2,1)S(1)}, bf16[320,6144]{1,0:T(8,128)(2,1)}, u32[]{:S(2)}) %copy-start.1) | copy-done | bytes 3932184
  16.3 4.5 %group_partial.1 = bf16[320,3072]{1,0:T(8,128)(2,1)S(1)} custom-call(s32[192]{0:T(256)S(1)} %copy-done.3, s32[192]{0:T(256)S(1)} %copy-done.4, s32[8]{0:T(128)S(1)} %copy-done.5, s32[2]{0:T(128)S(1)} %pad_add_fusion.refs_3_, bf16[24,128,128]{2,1,0:T(8,128)(2,1)S(1)} %bitcast.63, bf16[24,128,128]{2,1,0:T(8,128)(2,1)S(1)} %collective-permute-done.refs_5_, ...), custom_call_target="tpu_custom_call" | custom-call | tf_op jit(solution)/shard_map/group_partial/pallas_call | solution.py:52
  20.9 2.2 %collective-permute-start.1 = (bf16[40,3072]{1,0:T(8,128)(2,1)S(1)}, bf16[40,3072]{1,0:T(8,128)(2,1)S(1)}, u32[]{:S(2)}, u32[]{:S(2)}) collective-permute-start(bf16[40,3072]{1,0:T(8,128)(2,1)S(1)} %get-tuple-element.9), channel_id=1, source_target_pairs={{0,2},{2,4},{4,6},{6,0},{1,3},{3,5},{5,7},{7,1},{8,10},{10,12},{12... | collective-permute-start | bytes 737288 | tf_op jit(solution)/shard_map/ppermute | solution.py:79
  23.2 3.8 %collective-permute-start.3 = (bf16[40,3072]{1,0:T(8,128)(2,1)S(1)}, bf16[40,3072]{1,0:T(8,128)(2,1)S(1)}, u32[]{:S(2)}, u32[]{:S(2)}) collective-permute-start(bf16[40,3072]{1,0:T(8,128)(2,1)S(1)} %get-tuple-element.11), channel_id=1, source_target_pairs={{0,6},{2,0},{4,2},{6,4},{1,7},{3,1},{5,3},{7,5},{8,14},{10,8},{12,... | collective-permute-start | bytes 737288 | tf_op jit(solution)/shard_map/ppermute | solution.py:79
  26.9 3.6 %collective-permute-done.1 = bf16[40,3072]{1,0:T(8,128)(2,1)S(1)} collective-permute-done((bf16[40,3072]{1,0:T(8,128)(2,1)S(1)}, bf16[40,3072]{1,0:T(8,128)(2,1)S(1)}, u32[]{:S(2)}, u32[]{:S(2)}) %collective-permute-start.1) | collective-permute-done | bytes 245792 | tf_op jit(solution)/shard_map/ppermute | solution.py:79
  30.5 2.4 %collective-permute-done.3 = bf16[40,3072]{1,0:T(8,128)(2,1)S(1)} collective-permute-done((bf16[40,3072]{1,0:T(8,128)(2,1)S(1)}, bf16[40,3072]{1,0:T(8,128)(2,1)S(1)}, u32[]{:S(2)}, u32[]{:S(2)}) %collective-permute-start.3) | collective-permute-done | bytes 245792 | tf_op jit(solution)/shard_map/ppermute | solution.py:79
  33.1 4.1 %collective-permute-start.2 = (bf16[80,3072]{1,0:T(8,128)(2,1)S(1)}, bf16[80,3072]{1,0:T(8,128)(2,1)S(1)}, u32[]{:S(2)}, u32[]{:S(2)}) collective-permute-start(bf16[80,3072]{1,0:T(8,128)(2,1)S(1)} %pad_maximum_fusion.3), channel_id=1, source_target_pairs={{0,2},{2,4},{4,6},{6,0},{1,3},{3,5},{5,7},{7,1},{8,10},{10,12},{12... | collective-permute-start | bytes 1474568 | tf_op jit(solution)/shard_map/ppermute | solution.py:79
  39.9 7.4 %collective-permute-done.2 = bf16[80,3072]{1,0:T(8,128)(2,1)S(1)} collective-permute-done((bf16[80,3072]{1,0:T(8,128)(2,1)S(1)}, bf16[80,3072]{1,0:T(8,128)(2,1)S(1)}, u32[]{:S(2)}, u32[]{:S(2)}) %collective-permute-start.2) | collective-permute-done | bytes 491552 | tf_op jit(solution)/shard_map/ppermute | solution.py:79
  47.2 4.4 %collective-permute-done.4 = bf16[80,3072]{1,0:T(8,128)(2,1)} collective-permute-done((bf16[80,3072]{1,0:T(8,128)(2,1)}, bf16[80,3072]{1,0:T(8,128)(2,1)}, u32[]{:S(2)}, u32[]{:S(2)}) %collective-permute-start.4) | collective-permute-done | bytes 491552 | tf_op jit(solution)/shard_map/ppermute | solution.py:79
  54.8 18.8 %all-to-all-start = ((bf16[64,30,128]{2,1,0:T(8,128)(2,1)}), bf16[64,30,128]{2,1,0:T(8,128)(2,1)S(1)}, u32[]{:S(2)}, u32[]{:S(2)}) async-start(bf16[64,30,128]{2,1,0:T(8,128)(2,1)} %copy.17), calls=%async_computation | async-start | bytes 1048576 | tf_op jit(solution)/shard_map/all_to_all | solution.py:151
  74.3 28.3 %all-to-all-done = bf16[64,30,128]{2,1,0:T(8,128)(2,1)S(1)} async-done(((bf16[64,30,128]{2,1,0:T(8,128)(2,1)}), bf16[64,30,128]{2,1,0:T(8,128)(2,1)S(1)}, u32[]{:S(2)}, u32[]{:S(2)}) %all-to-all-start) | async-done | bytes 491552 | tf_op jit(solution)/shard_map/all_to_all | solution.py:151
  103.2 3.3 %collective-permute-start.6 = (bf16[320,768]{1,0:T(8,128)(2,1)S(1)}, bf16[320,768]{1,0:T(8,128)(2,1)S(1)}, u32[]{:S(2)}, u32[]{:S(2)}) collective-permute-start(bf16[320,768]{1,0:T(8,128)(2,1)S(1)} %bitcast.72), channel_id=1, source_target_pairs={{0,2},{2,4},{4,6},{6,0},{1,3},{3,5},{5,7},{7,1},{8,10},{10,12},{12... | collective-permute-start | bytes 1474568 | tf_op jit(solution)/shard_map/ppermute | solution.py:79
  106.5 2.6 %collective-permute-start.5 = (bf16[320,768]{1,0:T(8,128)(2,1)S(1)}, bf16[320,768]{1,0:T(8,128)(2,1)S(1)}, u32[]{:S(2)}, u32[]{:S(2)}) collective-permute-start(bf16[320,768]{1,0:T(8,128)(2,1)S(1)} %bitcast.73), channel_id=1, source_target_pairs={{0,6},{2,0},{4,2},{6,4},{1,7},{3,1},{5,3},{7,5},{8,14},{10,8},{12,... | collective-permute-start | bytes 1474568 | tf_op jit(solution)/shard_map/ppermute | solution.py:79
  109.1 6.1 %collective-permute-done.6 = bf16[320,768]{1,0:T(8,128)(2,1)S(1)} collective-permute-done((bf16[320,768]{1,0:T(8,128)(2,1)S(1)}, bf16[320,768]{1,0:T(8,128)(2,1)S(1)}, u32[]{:S(2)}, u32[]{:S(2)}) %collective-permute-start.6) | collective-permute-done | bytes 491552 | tf_op jit(solution)/shard_map/ppermute | solution.py:79
  115.2 3.7 %collective-permute-start.7 = (bf16[160,768]{1,0:T(8,128)(2,1)S(1)}, bf16[160,768]{1,0:T(8,128)(2,1)S(1)}, u32[]{:S(2)}, u32[]{:S(2)}) collective-permute-start(bf16[160,768]{1,0:T(8,128)(2,1)S(1)} %slice.74), channel_id=1, source_target_pairs={{0,2},{2,4},{4,6},{6,0},{1,3},{3,5},{5,7},{7,1},{8,10},{10,12},{12... | collective-permute-start | bytes 737288 | tf_op jit(solution)/shard_map/ppermute | solution.py:79
  123.3 3.8 %collective-permute-done.8 = bf16[160,768]{1,0:T(8,128)(2,1)S(1)} collective-permute-done((bf16[160,768]{1,0:T(8,128)(2,1)S(1)}, bf16[160,768]{1,0:T(8,128)(2,1)S(1)}, u32[]{:S(2)}, u32[]{:S(2)}) %collective-permute-start.8) | collective-permute-done | bytes 245792 | tf_op jit(solution)/shard_map/ppermute | solution.py:79
  130.6 20.8 %all-gather.2.cloned.1.call-done = bf16[1536,720]{1,0:T(8,128)(2,1)} async-done(((bf16[96,720]{1,0:T(8,128)(2,1)}), bf16[1536,720]{1,0:T(8,128)(2,1)}) %all-gather.2.cloned.1.call-update) | async-done | bytes 2211856 | tf_op jit(solution)/shard_map/all_gather | solution.py:128
  156.3 3.0 %collective-permute-start.10 = (bf16[160,720]{1,0:T(8,128)(2,1)S(1)}, bf16[160,720]{1,0:T(8,128)(2,1)S(1)}, u32[]{:S(2)}, u32[]{:S(2)}) collective-permute-start(bf16[160,720]{1,0:T(8,128)(2,1)S(1)} %get-tuple-element.13), channel_id=1, source_target_pairs={{0,128},{128,256},{256,384},{384,0},{1,129},{129,257},{257,385},{3... | collective-permute-start | bytes 691208 | tf_op jit(solution)/shard_map/ppermute | solution.py:79
  160.3 2.8 %collective-permute-start.12 = (bf16[160,720]{1,0:T(8,128)(2,1)S(1)}, bf16[160,720]{1,0:T(8,128)(2,1)S(1)}, u32[]{:S(2)}, u32[]{:S(2)}) collective-permute-start(bf16[160,720]{1,0:T(8,128)(2,1)S(1)} %get-tuple-element.14), channel_id=1, source_target_pairs={{0,384},{128,0},{256,128},{384,256},{1,385},{129,1},{257,129},{385... | collective-permute-start | bytes 691208 | tf_op jit(solution)/shard_map/ppermute | solution.py:79
  164.1 2.9 %collective-permute-done.10 = bf16[160,720]{1,0:T(8,128)(2,1)S(1)} collective-permute-done((bf16[160,720]{1,0:T(8,128)(2,1)S(1)}, bf16[160,720]{1,0:T(8,128)(2,1)S(1)}, u32[]{:S(2)}, u32[]{:S(2)}) %collective-permute-start.10) | collective-permute-done | bytes 230432 | tf_op jit(solution)/shard_map/ppermute | solution.py:79
  167.9 4.2 %collective-permute-start.11 = (bf16[320,720]{1,0:T(8,128)(2,1)}, bf16[320,720]{1,0:T(8,128)(2,1)}, u32[]{:S(2)}, u32[]{:S(2)}) collective-permute-start(bf16[320,720]{1,0:T(8,128)(2,1)} %pad_maximum_fusion.5), channel_id=1, source_target_pairs={{0,128},{128,256},{256,384},{384,0},{1,129},{129,257},{257,385},{3... | collective-permute-start | bytes 1382408 | tf_op jit(solution)/shard_map/ppermute | solution.py:79
  175.0 4.0 %collective-permute-done.11 = bf16[320,720]{1,0:T(8,128)(2,1)} collective-permute-done((bf16[320,720]{1,0:T(8,128)(2,1)}, bf16[320,720]{1,0:T(8,128)(2,1)}, u32[]{:S(2)}, u32[]{:S(2)}) %collective-permute-start.11) | collective-permute-done | bytes 460832 | tf_op jit(solution)/shard_map/ppermute | solution.py:79
  179.0 6.3 %collective-permute-done.13 = bf16[320,720]{1,0:T(8,128)(2,1)} collective-permute-done((bf16[320,720]{1,0:T(8,128)(2,1)}, bf16[320,720]{1,0:T(8,128)(2,1)}, u32[]{:S(2)}, u32[]{:S(2)}) %collective-permute-start.13) | collective-permute-done | bytes 460832 | tf_op jit(solution)/shard_map/ppermute | solution.py:79
  185.3 2.4 %fusion.3 = bf16[320,720]{1,0:T(8,128)(2,1)S(1)} fusion(bf16[320,720]{1,0:T(8,128)(2,1)} %collective-permute-done.13, bf16[320,720]{1,0:T(8,128)(2,1)} %collective-permute-done.11, bf16[4,320,1536]{2,1,0:T(8,128)(2,1)} %copy-done.6, s32[]{:T(128)S(6)} %select_n.36, bf16[768,720]{1,0:T(8,128)(2,1)S(1)} %copy-done.8, bf16[768,720]{1,0:T(8,128)(2,1)S(1)} %get-tuple-element.5), kind=kOutput, calls=%fused_computation.11 | convolution fusion | flops 713825280 | bytes 4638724 | tf_op jit(solution)/shard_map/dot_general | solution.py:161
  (62 shorter events, 34.4 us)
Async XLA Ops:
  6.5 181.2 %copy-start = (bf16[64,64]{1,0:T(8,128)(2,1)S(1)}, bf16[64,64]{1,0:T(8,128)(2,1)}, u32[]{:S(2)}) copy-start(bf16[64,64]{1,0:T(8,128)(2,1)} %param.11) | copy-start | bytes 24580
  6.5 4.5 %collective-permute-start = (bf16[24,128,128]{2,1,0:T(8,128)(2,1)}, bf16[24,128,128]{2,1,0:T(8,128)(2,1)S(1)}, u32[]{:S(2)}, u32[]{:S(2)}) collective-permute-start(bf16[24,128,128]{2,1,0:T(8,128)(2,1)} %bitcast.62), channel_id=1, source_target_pairs={{0,1},{1,0},{2,3},{3,2},{4,5},{5,4},{6,7},{7,6},{8,9},{9,8},{10,11... | collective-permute-start | bytes 2359304 | tf_op jit(solution)/shard_map/ppermute | solution.py:79
  11.0 2.1 %copy-start.1 = (bf16[320,6144]{1,0:T(8,128)(2,1)S(1)}, bf16[320,6144]{1,0:T(8,128)(2,1)}, u32[]{:S(2)}) copy-start(bf16[320,6144]{1,0:T(8,128)(2,1)} %refs_6_.1) | copy-start | bytes 11796484
  13.2 1.1 copy-start.2
  14.3 0.7 copy-start.3
  15.0 0.7 copy-start.4
  20.9 9.6 %collective-permute-start.1 = (bf16[40,3072]{1,0:T(8,128)(2,1)S(1)}, bf16[40,3072]{1,0:T(8,128)(2,1)S(1)}, u32[]{:S(2)}, u32[]{:S(2)}) collective-permute-start(bf16[40,3072]{1,0:T(8,128)(2,1)S(1)} %get-tuple-element.9), channel_id=1, source_target_pairs={{0,2},{2,4},{4,6},{6,0},{1,3},{3,5},{5,7},{7,1},{8,10},{10,12},{12... | collective-permute-start | bytes 737288 | tf_op jit(solution)/shard_map/ppermute | solution.py:79
  23.2 9.8 %collective-permute-start.3 = (bf16[40,3072]{1,0:T(8,128)(2,1)S(1)}, bf16[40,3072]{1,0:T(8,128)(2,1)S(1)}, u32[]{:S(2)}, u32[]{:S(2)}) collective-permute-start(bf16[40,3072]{1,0:T(8,128)(2,1)S(1)} %get-tuple-element.11), channel_id=1, source_target_pairs={{0,6},{2,0},{4,2},{6,4},{1,7},{3,1},{5,3},{7,5},{8,14},{10,8},{12,... | collective-permute-start | bytes 737288 | tf_op jit(solution)/shard_map/ppermute | solution.py:79
  33.1 14.2 %collective-permute-start.2 = (bf16[80,3072]{1,0:T(8,128)(2,1)S(1)}, bf16[80,3072]{1,0:T(8,128)(2,1)S(1)}, u32[]{:S(2)}, u32[]{:S(2)}) collective-permute-start(bf16[80,3072]{1,0:T(8,128)(2,1)S(1)} %pad_maximum_fusion.3), channel_id=1, source_target_pairs={{0,2},{2,4},{4,6},{6,0},{1,3},{3,5},{5,7},{7,1},{8,10},{10,12},{12... | collective-permute-start | bytes 1474568 | tf_op jit(solution)/shard_map/ppermute | solution.py:79
  38.0 13.7 %collective-permute-start.4 = (bf16[80,3072]{1,0:T(8,128)(2,1)}, bf16[80,3072]{1,0:T(8,128)(2,1)}, u32[]{:S(2)}, u32[]{:S(2)}) collective-permute-start(bf16[80,3072]{1,0:T(8,128)(2,1)} %pad_maximum_fusion.4), channel_id=1, source_target_pairs={{0,6},{2,0},{4,2},{6,4},{1,7},{3,1},{5,3},{7,5},{8,14},{10,8},{12,... | collective-permute-start | bytes 1474568 | tf_op jit(solution)/shard_map/ppermute | solution.py:79
  54.8 47.8 %all-to-all-start = ((bf16[64,30,128]{2,1,0:T(8,128)(2,1)}), bf16[64,30,128]{2,1,0:T(8,128)(2,1)S(1)}, u32[]{:S(2)}, u32[]{:S(2)}) async-start(bf16[64,30,128]{2,1,0:T(8,128)(2,1)} %copy.17), calls=%async_computation | async-start | bytes 1048576 | tf_op jit(solution)/shard_map/all_to_all | solution.py:151
  73.6 77.8 %all-gather.2.cloned.1.call-start = ((), (), s32[]{:S(2)}) async-start(), calls=%async_computation.1 | async-start | bytes 2506752 | tf_op jit(solution)/shard_map/all_gather | solution.py:128
  103.2 12.0 %collective-permute-start.6 = (bf16[320,768]{1,0:T(8,128)(2,1)S(1)}, bf16[320,768]{1,0:T(8,128)(2,1)S(1)}, u32[]{:S(2)}, u32[]{:S(2)}) collective-permute-start(bf16[320,768]{1,0:T(8,128)(2,1)S(1)} %bitcast.72), channel_id=1, source_target_pairs={{0,2},{2,4},{4,6},{6,0},{1,3},{3,5},{5,7},{7,1},{8,10},{10,12},{12... | collective-permute-start | bytes 1474568 | tf_op jit(solution)/shard_map/ppermute | solution.py:79
  106.5 12.5 %collective-permute-start.5 = (bf16[320,768]{1,0:T(8,128)(2,1)S(1)}, bf16[320,768]{1,0:T(8,128)(2,1)S(1)}, u32[]{:S(2)}, u32[]{:S(2)}) collective-permute-start(bf16[320,768]{1,0:T(8,128)(2,1)S(1)} %bitcast.73), channel_id=1, source_target_pairs={{0,6},{2,0},{4,2},{6,4},{1,7},{3,1},{5,3},{7,5},{8,14},{10,8},{12,... | collective-permute-start | bytes 1474568 | tf_op jit(solution)/shard_map/ppermute | solution.py:79
  115.2 8.1 %collective-permute-start.7 = (bf16[160,768]{1,0:T(8,128)(2,1)S(1)}, bf16[160,768]{1,0:T(8,128)(2,1)S(1)}, u32[]{:S(2)}, u32[]{:S(2)}) collective-permute-start(bf16[160,768]{1,0:T(8,128)(2,1)S(1)} %slice.74), channel_id=1, source_target_pairs={{0,2},{2,4},{4,6},{6,0},{1,3},{3,5},{5,7},{7,1},{8,10},{10,12},{12... | collective-permute-start | bytes 737288 | tf_op jit(solution)/shard_map/ppermute | solution.py:79
  119.0 8.1 %collective-permute-start.8 = (bf16[160,768]{1,0:T(8,128)(2,1)S(1)}, bf16[160,768]{1,0:T(8,128)(2,1)S(1)}, u32[]{:S(2)}, u32[]{:S(2)}) collective-permute-start(bf16[160,768]{1,0:T(8,128)(2,1)S(1)} %slice.75), channel_id=1, source_target_pairs={{0,6},{2,0},{4,2},{6,4},{1,7},{3,1},{5,3},{7,5},{8,14},{10,8},{12,... | collective-permute-start | bytes 737288 | tf_op jit(solution)/shard_map/ppermute | solution.py:79
  128.7 24.5 %collective-permute-start.9 = (bf16[4,320,768]{2,1,0:T(8,128)(2,1)}, bf16[4,320,768]{2,1,0:T(8,128)(2,1)}, u32[]{:S(2)}, u32[]{:S(2)}) collective-permute-start(bf16[4,320,768]{2,1,0:T(8,128)(2,1)} %pad_maximum_fusion.2), channel_id=1, source_target_pairs={{0,1},{1,0},{2,3},{3,2},{4,5},{5,4},{6,7},{7,6},{8,9},{9,8},{10,11... | collective-permute-start | bytes 5898248 | tf_op jit(solution)/shard_map/ppermute | solution.py:79
  153.2 9.9 %copy-start.7 = (bf16[768,720]{1,0:T(8,128)(2,1)}, bf16[768,720]{1,0:T(8,128)(2,1)S(1)}, u32[]{:S(2)}) copy-start(bf16[768,720]{1,0:T(8,128)(2,1)S(1)} %get-tuple-element.6) | copy-start | bytes 3317764
  155.3 7.8 %copy-start.6 = (bf16[4,320,1536]{2,1,0:T(8,128)(2,1)}, bf16[4,320,1536]{2,1,0:T(8,128)(2,1)S(1)}, u32[]{:S(2)}) copy-start(bf16[4,320,1536]{2,1,0:T(8,128)(2,1)S(1)} %pad_maximum_fusion) | copy-start | bytes 11796484
  156.3 10.7 %collective-permute-start.10 = (bf16[160,720]{1,0:T(8,128)(2,1)S(1)}, bf16[160,720]{1,0:T(8,128)(2,1)S(1)}, u32[]{:S(2)}, u32[]{:S(2)}) collective-permute-start(bf16[160,720]{1,0:T(8,128)(2,1)S(1)} %get-tuple-element.13), channel_id=1, source_target_pairs={{0,128},{128,256},{256,384},{384,0},{1,129},{129,257},{257,385},{3... | collective-permute-start | bytes 691208 | tf_op jit(solution)/shard_map/ppermute | solution.py:79
  160.3 11.9 %collective-permute-start.12 = (bf16[160,720]{1,0:T(8,128)(2,1)S(1)}, bf16[160,720]{1,0:T(8,128)(2,1)S(1)}, u32[]{:S(2)}, u32[]{:S(2)}) collective-permute-start(bf16[160,720]{1,0:T(8,128)(2,1)S(1)} %get-tuple-element.14), channel_id=1, source_target_pairs={{0,384},{128,0},{256,128},{384,256},{1,385},{129,1},{257,129},{385... | collective-permute-start | bytes 691208 | tf_op jit(solution)/shard_map/ppermute | solution.py:79
  164.1 21.2 %copy-start.8 = (bf16[768,720]{1,0:T(8,128)(2,1)S(1)}, bf16[768,720]{1,0:T(8,128)(2,1)}, u32[]{:S(2)}) copy-start(bf16[768,720]{1,0:T(8,128)(2,1)} %copy-done.7) | copy-start | bytes 3317764
  167.9 11.0 %collective-permute-start.11 = (bf16[320,720]{1,0:T(8,128)(2,1)}, bf16[320,720]{1,0:T(8,128)(2,1)}, u32[]{:S(2)}, u32[]{:S(2)}) collective-permute-start(bf16[320,720]{1,0:T(8,128)(2,1)} %pad_maximum_fusion.5), channel_id=1, source_target_pairs={{0,128},{128,256},{256,384},{384,0},{1,129},{129,257},{257,385},{3... | collective-permute-start | bytes 1382408 | tf_op jit(solution)/shard_map/ppermute | solution.py:79
  173.0 12.2 %collective-permute-start.13 = (bf16[320,720]{1,0:T(8,128)(2,1)}, bf16[320,720]{1,0:T(8,128)(2,1)}, u32[]{:S(2)}, u32[]{:S(2)}) collective-permute-start(bf16[320,720]{1,0:T(8,128)(2,1)} %pad_maximum_fusion.6), channel_id=1, source_target_pairs={{0,384},{128,0},{256,128},{384,256},{1,385},{129,1},{257,129},{385... | collective-permute-start | bytes 1382408 | tf_op jit(solution)/shard_map/ppermute | solution.py:79
  (1 other events, 0.7 us)
Sparse Core Ops, SparseCore 0:
  76.5 74.8 all-gather.1

commit v2 on v1

v2 whole, which is shorter than its diff:
```python
import jax
import jax.numpy as jnp
from jax import lax
from jax.experimental import pallas as pl
from jax.experimental.pallas import tpu as pltpu
from jax.sharding import Mesh, PartitionSpec as P

GROUP_ROWS = 6


def partial_kernel(
    rows, cols, counts, place, own, other, occ, order, out, total, coef, *, slots, width, blocks_x
):
    y, core = place[0], place[1]
    occ_width = occ.shape[0]
    half_blocks = blocks_x // 2
    pick = lax.broadcasted_iota(jnp.int32, (occ_width, occ_width), 1) == order[...]
    pick = jnp.where(pick, 1.0, 0.0).astype(jnp.bfloat16)
    for row in range(coef.shape[0]):
        chosen = jnp.dot(
            pick, occ[:, row * width : (row + 1) * width], preferred_element_type=jnp.float32
        )
        coef[row] = chosen.astype(jnp.bfloat16)
    total[...] = jnp.zeros_like(total)

    for which, blocks in ((core, own), (1 - core, other)):
        group = 2 * y + which

        @pl.loop(0, counts[group])
        def _(slot):
            col = cols[group * slots + slot]
            inside = lax.rem(col, blocks_x)

            @pl.when(inside // half_blocks == core)
            def _():
                row = rows[group * slots + slot] - 2 * y * GROUP_ROWS
                local = (col // blocks_x) * half_blocks + lax.rem(inside, half_blocks)
                total[local] += jnp.dot(
                    coef[row], blocks[slot], preferred_element_type=jnp.float32
                )

    ny, nx, rows_y, _ = out.shape
    for block in range(total.shape[0]):
        at = block // half_blocks, block % half_blocks * width
        for part in range(ny):
            out[part, at[0], :, at[1] : at[1] + width] = total[
                block, part * rows_y : (part + 1) * rows_y
            ].astype(out.dtype)


def group_partial(own, other, occ_coef, order, rows, cols, counts, place, nx, ny):
    slots, width = own.shape[0], own.shape[1]
    occ_width, ao_width = occ_coef.shape
    half_blocks = ao_width // width // 2
    blocks_x = ao_width // width // nx
    shape = (ny, nx, occ_width // ny, blocks_x // 2 * width)
    kernel = lambda *refs: partial_kernel(*refs, slots=slots, width=width, blocks_x=blocks_x)
    whole = lambda *shape: pl.BlockSpec(shape, lambda i, *_: (0,) * len(shape))
    return pl.pallas_call(
        kernel,
        grid_spec=pltpu.PrefetchScalarGridSpec(
            num_scalar_prefetch=4,
            grid=(1,),
            in_specs=[
                whole(slots, width, width),
                whole(slots, width, width),
                pl.BlockSpec(
                    (occ_width, 2 * GROUP_ROWS * width), lambda i, r, c, n, place: (0, place[0])
                ),
                whole(occ_width, 1),
            ],
            out_specs=whole(*shape),
            scratch_shapes=[
                pltpu.VMEM((half_blocks, occ_width, width), jnp.float32),
                pltpu.VMEM((2 * GROUP_ROWS, occ_width, width), jnp.bfloat16),
            ],
        ),
        out_shape=jax.ShapeDtypeStruct(shape, jnp.bfloat16),
        compiler_params=pltpu.CompilerParams(vmem_limit_bytes=60 << 20),
        name="group_partial",
    )(rows, cols, counts, place, own, other, occ_coef, order)


def shift(value, axis, step):
    n = lax.axis_size(axis)
    return lax.ppermute(value, axis, [(i, (i + step) % n) for i in range(n)])


def swap(value, axis):
    return lax.all_to_all(value, axis, 0, 0, tiled=True)


def scatter_sum(terms, axis):
    return jnp.sum(swap(terms, axis).astype(jnp.float32), 0).astype(jnp.bfloat16)


def gather(mine, axis):
    n = lax.axis_size(axis)
    return swap(jnp.broadcast_to(mine[None], (n,) + mine.shape), axis)


def shards(
    pair_integrals,
    occ_coef,
    vir_coef,
    metric_factor,
    block_rows,
    block_cols,
    block_count,
    occ_order,
):
    x, y, core = lax.axis_index("x"), lax.axis_index("y"), lax.axis_index("c")
    nx, nz, ny = lax.axis_size("x"), lax.axis_size("z"), lax.axis_size("y")
    width = pair_integrals.shape[2]
    occ_width, ao_width = occ_coef.shape
    vir_width = vir_coef.shape[1]
    naux = nx * nz
    each = occ_width // naux
    blocks_x = ao_width // width // nx
    half_blocks = blocks_x // 2

    vir_rows = lax.all_gather(vir_coef, "z", axis=0, tiled=True)

    own = pair_integrals[0]
    other = shift(own, "c", 1)
    order = occ_order.reshape(nx, nz, each).transpose(0, 2, 1).reshape(occ_width, 1)
    place = jnp.stack([y, core]).astype(jnp.int32)
    part = group_partial(
        own, other, occ_coef, order, block_rows, block_cols, block_count, place, nx, ny
    )
    share = scatter_sum(part, "y")
    share = swap(share, "x")
    send = share.reshape(nx, each, nz, half_blocks, width).transpose(2, 0, 1, 3, 4)
    got = swap(send.reshape(nz, nx * each * half_blocks, width), "z")
    got, vir_rows = lax.optimization_barrier((got, vir_rows))
    mine = got.reshape(nz, nx, each, half_blocks, width).transpose(2, 1, 0, 3, 4)
    mine = mine.reshape(each * naux, half_blocks * width)
    held = gather(mine, "y")
    traded = shift(held, "c", 1)
    deep = vir_rows.shape[0] // 2
    terms = jnp.einsum(
        "xmk,kv->xmv",
        held,
        lax.dynamic_slice_in_dim(vir_rows, core * deep, deep, 0),
        preferred_element_type=jnp.float32,
    ) + jnp.einsum(
        "xmk,kv->xmv",
        traded,
        lax.dynamic_slice_in_dim(vir_rows, (1 - core) * deep, deep, 0),
        preferred_element_type=jnp.float32,
    )
    pencil = scatter_sum(terms.astype(jnp.bfloat16), "x").reshape(each, naux, vir_width)
    mixed = jnp.einsum(
        "qp,kpv->qkv", metric_factor, pencil, preferred_element_type=jnp.float32
    )
    return mixed.astype(jnp.bfloat16)


def solution(mesh):
    aux, ao = mesh.devices.shape
    grid = Mesh(mesh.devices.reshape(4, aux // 4, ao // 2, 2), ("x", "z", "y", "c"))
    every = P()
    return jax.shard_map(
        shards,
        mesh=grid,
        in_specs=(P(("x", "z"), ("y", "c")), every, P(("x", "z"), ("y", "c"))) + (every,) * 5,
        out_specs=P(None, ("x", "z"), ("y", "c")),
        check_vma=False,
    )
```

time: 197 us -> 180 us (0.914)
  the two profiles are of different devices: /device:TPU:22 before, /device:TPU:32 now
where the time goes in v2:
time: 180 us
  blocking collectives  97.4 us (54%)
  waiting for transfers between devices  24.1 us (13%)
  starting transfers between devices  19.2 us (11%)
  between operations  13.5 us (8%)
  Pallas kernels  8.36 us (5%)
  matrix products  8.17 us (5%)
  local copies, waits for them, and re-layouts  7.09 us (4%)
    all_to_all x4, blocking collectives, swap(): return lax.all_to_all(value, axis, 0, 0, tiled=True)  97.4 us
    all_gather x1, waiting for transfers between devices, shards(): vir_rows = lax.all_gather(vir_coef, 'z', axis=0, tiled=True)  19.9 us
    all_to_all x1, starting transfers between devices, swap(): return lax.all_to_all(value, axis, 0, 0, tiled=True)  15.2 us
    pallas_call x1, Pallas kernels, group_partial(): pl.pallas_call(kernel, grid_spec=pltpu.PrefetchScalarGridSpec(num_scalar_...  8.36 us
    all_to_all x1, waiting for transfers between devices, swap(): return lax.all_to_all(value, axis, 0, 0, tiled=True)  4.06 us
    ppermute x2, starting transfers between devices, shift(): return lax.ppermute(value, axis, [(i, (i + step) % n) for i in range(n)])  3.95 us
    dot_general x1, matrix products, shards(): jnp.einsum('xmk,kv->xmv', held, lax.dynamic_slice_in_dim(vir_rows, core *...  3.73 us
  transfers between devices with their start and end apart: 4, of which 3 were waited for; matrix products, arithmetic and copies ran while one was open for 6% of the time, Pallas kernels for 5%

profile of v2, /device:TPU:32, one launch (start us, length us, event | category | flops | bytes accessed | tf_op | source)
XLA Modules:
  0.0 179.6 jit_solution(18046130586143680227)
XLA Ops:
  6.5 2.0 %collective-permute-start = (bf16[24,128,128]{2,1,0:T(8,128)(2,1)}, bf16[24,128,128]{2,1,0:T(8,128)(2,1)S(1)}, u32[]{:S(2)}, u32[]{:S(2)}) collective-permute-start(bf16[24,128,128]{2,1,0:T(8,128)(2,1)} %bitcast.35), channel_id=1, source_target_pairs={{0,1},{1,0},{2,3},{3,2},{4,5},{5,4},{6,7},{7,6},{8,9},{9,8},{10,11... | collective-permute-start | bytes 2359304 | tf_op jit(solution)/shard_map/ppermute | solution.py:86
  8.6 0.8 reshape.19
  9.5 0.8 reshape.28.refs_7_
  10.3 0.6 pad_add_fusion.refs_3_
  11.1 0.9 copy-done.3
  11.9 8.4 %group_partial.1 = bf16[4,4,80,768]{3,2,1,0:T(8,128)(2,1)} custom-call(s32[192]{0:T(256)} %refs_0_.1, s32[192]{0:T(256)} %refs_1_.1, s32[8]{0:T(128)} %refs_2_.1, s32[2]{0:T(128)} %pad_add_fusion.refs_3_, bf16[24,128,128]{2,1,0:T(8,128)(2,1)} %bitcast.36, bf16[24,128,128]{2,1,0:T(8,128)(2,1)} %copy-done.3, bf16[320,6144]{1,0:T(8,128)(2,1)} %refs_6_.1, ...), custom_call_target="tpu_custom_call" | custom-call | tf_op jit(solution)/shard_map/group_partial/pallas_call | solution.py:59
  20.3 29.1 %all_to_all.25 = bf16[4,4,80,768]{3,2,1,0:T(8,128)(2,1)S(1)} all-to-all(bf16[4,4,80,768]{3,2,1,0:T(8,128)(2,1)} %group_partial.1), channel_id=1, replica_groups=mesh['x'=4,'z'=16,'y'=4,'c'=2] {'y'}, dimensions={0} | all-to-all | bytes 3932160 | tf_op jit(solution)/shard_map/all_to_all | solution.py:90
  49.4 0.5 reduce_sum.24
  49.9 12.6 %all_to_all.26 = bf16[4,80,768]{2,1,0:T(8,128)(2,1)S(1)} all-to-all(bf16[4,80,768]{2,1,0:T(8,128)(2,1)S(1)} %reduce_sum.24), channel_id=1, replica_groups=mesh['x'=4,'z'=16,'y'=4,'c'=2] {'x'}, dimensions={0} | all-to-all | bytes 983040 | tf_op jit(solution)/shard_map/all_to_all | solution.py:90
  62.5 0.6 reshape.21
  63.2 0.9 copy.18
  64.1 15.2 %all-to-all-start.2 = ((bf16[16,120,128]{2,1,0:T(8,128)(2,1)}), bf16[16,120,128]{2,1,0:T(8,128)(2,1)S(1)}, u32[]{:S(2)}, u32[]{:S(2)}) async-start(bf16[16,120,128]{2,1,0:T(8,128)(2,1)} %copy.18), calls=%async_computation.2 | async-start | bytes 983040 | tf_op jit(solution)/shard_map/all_to_all | solution.py:90
  79.3 19.9 %all-gather.2.cloned.1.call-done = bf16[1536,720]{1,0:T(8,128)(2,1)} async-done(((bf16[96,720]{1,0:T(8,128)(2,1)}), bf16[1536,720]{1,0:T(8,128)(2,1)}) %all-gather.2.cloned.1.call-update) | async-done | bytes 2211856 | tf_op jit(solution)/shard_map/all_gather | solution.py:122
  99.2 4.1 %all-to-all-done.2 = bf16[16,120,128]{2,1,0:T(8,128)(2,1)S(1)} async-done(((bf16[16,120,128]{2,1,0:T(8,128)(2,1)}), bf16[16,120,128]{2,1,0:T(8,128)(2,1)S(1)}, u32[]{:S(2)}, u32[]{:S(2)}) %all-to-all-start.2) | async-done | bytes 491552 | tf_op jit(solution)/shard_map/all_to_all | solution.py:90
  103.4 0.2 copy.20
  103.6 0.1 broadcast_in_dim.8
  103.8 26.4 %all_to_all.27 = bf16[4,320,768]{2,1,0:T(8,128)(2,1)} all-to-all(bf16[4,320,768]{2,1,0:T(8,128)(2,1)S(1)} %broadcast_in_dim.8), channel_id=1, replica_groups=mesh['x'=4,'z'=16,'y'=4,'c'=2] {'y'}, dimensions={0} | all-to-all | bytes 3932160 | tf_op jit(solution)/shard_map/all_to_all | solution.py:90
  130.1 1.9 %collective-permute-start.1 = (bf16[4,320,768]{2,1,0:T(8,128)(2,1)}, bf16[4,320,768]{2,1,0:T(8,128)(2,1)}, u32[]{:S(2)}, u32[]{:S(2)}) collective-permute-start(bf16[4,320,768]{2,1,0:T(8,128)(2,1)} %all_to_all.27), channel_id=1, source_target_pairs={{0,1},{1,0},{2,3},{3,2},{4,5},{5,4},{6,7},{7,6},{8,9},{9,8},{10,11... | collective-permute-start | bytes 5898248 | tf_op jit(solution)/shard_map/ppermute | solution.py:86
  132.1 2.5 %copy.21 = bf16[1536,720]{0,1:T(8,128)(2,1)} copy(bf16[1536,720]{1,0:T(8,128)(2,1)S(1)} %copy-done.1) | data formatting | bytes 4423680 | tf_op jit(solution)/shard_map/optimization_barrier | solution.py:135
  134.6 3.7 %fusion.2 = f32[4,320,720]{2,1,0:T(8,128)S(1)} fusion(bf16[4,320,768]{2,1,0:T(8,128)(2,1)} %all_to_all.27, bf16[1536,720]{0,1:T(8,128)(2,1)} %copy.21, s32[]{:T(128)S(6)} %select_n.6), kind=kOutput, calls=%fused_computation.4 | convolution fusion | flops 1415577600 | bytes 6758404 | tf_op jit(solution)/shard_map/xmk,kv->xmv/dot_general | solution.py:141
  138.3 3.4 %add_convert_fusion = bf16[4,320,720]{2,1,0:T(8,128)(2,1)S(1)} fusion(f32[4,320,720]{2,1,0:T(8,128)S(1)} %fusion.2, bf16[4,320,768]{2,1,0:T(8,128)(2,1)} %collective-permute-done.1, bf16[1536,720]{0,1:T(8,128)(2,1)S(1)} %copy-done.2, s32[]{:T(128)S(6)} %select_n.7), kind=kOutput, calls=%fused_computation | convolution fusion | flops 1417420800 | bytes 8847364 | tf_op jit(solution)/shard_map/xmk,kv->xmv/dot_general | solution.py:146
  141.7 29.4 %all_to_all.28 = bf16[4,320,720]{2,1,0:T(8,128)(2,1)S(1)} all-to-all(bf16[4,320,720]{2,1,0:T(8,128)(2,1)S(1)} %add_convert_fusion), channel_id=1, replica_groups=mesh['x'=4,'z'=16,'y'=4,'c'=2] {'x'}, dimensions={0} | all-to-all | bytes 3686400 | tf_op jit(solution)/shard_map/all_to_all | solution.py:90
  171.1 0.6 reduce_sum.25
  171.7 1.1 fusion
  (15 shorter events, 0.4 us)
Async XLA Ops:
  6.5 165.2 %copy-start = (bf16[64,64]{1,0:T(8,128)(2,1)S(1)}, bf16[64,64]{1,0:T(8,128)(2,1)}, u32[]{:S(2)}) copy-start(bf16[64,64]{1,0:T(8,128)(2,1)} %param.11) | copy-start | bytes 24580
  6.5 92.7 %all-gather.2.cloned.1.call-start = ((), (), s32[]{:S(2)}) async-start(), calls=%async_computation.5 | async-start | bytes 2506752 | tf_op jit(solution)/shard_map/all_gather | solution.py:122
  6.5 4.5 %collective-permute-start = (bf16[24,128,128]{2,1,0:T(8,128)(2,1)}, bf16[24,128,128]{2,1,0:T(8,128)(2,1)S(1)}, u32[]{:S(2)}, u32[]{:S(2)}) collective-permute-start(bf16[24,128,128]{2,1,0:T(8,128)(2,1)} %bitcast.35), channel_id=1, source_target_pairs={{0,1},{1,0},{2,3},{3,2},{4,5},{5,4},{6,7},{7,6},{8,9},{9,8},{10,11... | collective-permute-start | bytes 2359304 | tf_op jit(solution)/shard_map/ppermute | solution.py:86
  11.1 0.9 copy-start.3
  64.1 39.2 %all-to-all-start.2 = ((bf16[16,120,128]{2,1,0:T(8,128)(2,1)}), bf16[16,120,128]{2,1,0:T(8,128)(2,1)S(1)}, u32[]{:S(2)}, u32[]{:S(2)}) async-start(bf16[16,120,128]{2,1,0:T(8,128)(2,1)} %copy.18), calls=%async_computation.2 | async-start | bytes 983040 | tf_op jit(solution)/shard_map/all_to_all | solution.py:90
  103.8 28.3 %copy-start.1 = (bf16[1536,720]{1,0:T(8,128)(2,1)S(1)}, bf16[1536,720]{1,0:T(8,128)(2,1)}, u32[]{:S(2)}) copy-start(bf16[1536,720]{1,0:T(8,128)(2,1)} %all-gather.2.cloned.1.call-done) | copy-start | bytes 6635524
  130.1 8.2 %collective-permute-start.1 = (bf16[4,320,768]{2,1,0:T(8,128)(2,1)}, bf16[4,320,768]{2,1,0:T(8,128)(2,1)}, u32[]{:S(2)}, u32[]{:S(2)}) collective-permute-start(bf16[4,320,768]{2,1,0:T(8,128)(2,1)} %all_to_all.27), channel_id=1, source_target_pairs={{0,1},{1,0},{2,3},{3,2},{4,5},{5,4},{6,7},{7,6},{8,9},{9,8},{10,11... | collective-permute-start | bytes 5898248 | tf_op jit(solution)/shard_map/ppermute | solution.py:86
  134.6 3.8 %copy-start.2 = (bf16[1536,720]{0,1:T(8,128)(2,1)S(1)}, bf16[1536,720]{0,1:T(8,128)(2,1)}, u32[]{:S(2)}) copy-start(bf16[1536,720]{0,1:T(8,128)(2,1)} %copy.21) | copy-start | bytes 6635524
Sparse Core Ops, SparseCore 0:
  9.4 89.7 all-gather.1

commit v3 on v2

v3 whole, which is shorter than its diff:
```python
import jax
import jax.numpy as jnp
from jax import lax
from jax.experimental import pallas as pl
from jax.experimental.pallas import tpu as pltpu
from jax.sharding import Mesh, PartitionSpec as P

GROUP_ROWS = 6


def partial_kernel(rows, cols, counts, place, own, other, occ, order, out, total, coef):
    nx, ny, rows_y, half_width = out.shape
    slots, width = own.shape[:2]
    occ_width = occ.shape[0]
    half_blocks = half_width // width
    blocks_x = 2 * half_blocks
    y, core = place[0], place[1]
    pick = lax.broadcasted_iota(jnp.int32, (occ_width, occ_width), 1) == order[...]
    pick = jnp.where(pick, 1.0, 0.0).astype(jnp.bfloat16)
    for row in range(coef.shape[0]):
        chosen = jnp.dot(
            pick, occ[:, row * width : (row + 1) * width], preferred_element_type=jnp.float32
        )
        coef[row] = chosen.astype(coef.dtype)
    total[...] = jnp.zeros_like(total)

    for which, blocks in ((core, own), (1 - core, other)):
        group = 2 * y + which

        @pl.loop(0, counts[group])
        def _(slot):
            col = cols[group * slots + slot]
            inside = lax.rem(col, blocks_x)

            @pl.when(inside // half_blocks == core)
            def _():
                row = rows[group * slots + slot] - 2 * y * GROUP_ROWS
                local = (col // blocks_x) * half_blocks + lax.rem(inside, half_blocks)
                total[local] += jnp.dot(
                    coef[row], blocks[slot], preferred_element_type=jnp.float32
                )

    for block in range(total.shape[0]):
        at = block // half_blocks, block % half_blocks * width
        for part in range(ny):
            out[at[0], part, :, at[1] : at[1] + width] = total[
                block, part * rows_y : (part + 1) * rows_y
            ].astype(out.dtype)


def whole(*shape):
    return pl.BlockSpec(shape, lambda *_: (0,) * len(shape))


def group_partial(own, other, occ_coef, order, rows, cols, counts, place, nx, ny):
    slots, width = own.shape[0], own.shape[1]
    occ_width, ao_width = occ_coef.shape
    half_blocks = ao_width // width // 2
    chip_rows = 2 * GROUP_ROWS
    shape = (nx, ny, occ_width // ny, half_blocks // nx * width)
    return pl.pallas_call(
        partial_kernel,
        grid_spec=pltpu.PrefetchScalarGridSpec(
            num_scalar_prefetch=4,
            grid=(1,),
            in_specs=[
                whole(slots, width, width),
                whole(slots, width, width),
                pl.BlockSpec((occ_width, chip_rows * width), lambda i, r, c, n, place: (0, place[0])),
                whole(occ_width, 1),
            ],
            out_specs=whole(*shape),
            scratch_shapes=[
                pltpu.VMEM((half_blocks, occ_width, width), jnp.float32),
                pltpu.VMEM((chip_rows, occ_width, width), jnp.bfloat16),
            ],
        ),
        out_shape=jax.ShapeDtypeStruct(shape, jnp.bfloat16),
        compiler_params=pltpu.CompilerParams(vmem_limit_bytes=60 << 20),
        name="group_partial",
    )(rows, cols, counts, place, own, other, occ_coef, order)


def halves_kernel(place, rows, out, done):
    half = rows.shape[0] // 2
    copies = []
    for part, which in enumerate((place[1], 1 - place[1])):
        source = rows.at[pl.ds(pl.multiple_of(which * half, half), half)]
        copies.append(
            pltpu.make_async_copy(source, out.at[pl.ds(part * half, half)], done.at[part])
        )
    for copy in copies:
        copy.start()
    for copy in copies:
        copy.wait()


def halves(rows, place):
    return pl.pallas_call(
        halves_kernel,
        grid_spec=pltpu.PrefetchScalarGridSpec(
            num_scalar_prefetch=1,
            grid=(1,),
            in_specs=[pl.BlockSpec(memory_space=pl.ANY)],
            out_specs=whole(*rows.shape),
            scratch_shapes=[pltpu.SemaphoreType.DMA((2,))],
        ),
        out_shape=jax.ShapeDtypeStruct(rows.shape, rows.dtype),
        compiler_params=pltpu.CompilerParams(vmem_limit_bytes=16 << 20),
        cost_estimate=pl.CostEstimate(flops=0, bytes_accessed=4 << 20, transcendentals=0),
        name="vir_halves",
    )(place, rows)


def product_kernel(held, traded, coef, out):
    half, cut = held.shape[2], coef.shape[1]
    total = jnp.dot(held[0], coef[:half], preferred_element_type=jnp.float32)
    total += jnp.dot(traded[0], coef[half:], preferred_element_type=jnp.float32)
    out[0, :, :cut] = total.astype(out.dtype)
    if cut < out.shape[2]:
        out[0, :, cut:] = jnp.zeros((total.shape[0], out.shape[2] - cut), out.dtype)


def product(held, traded, coef, lanes):
    n, rows, half = held.shape
    width = pl.cdiv(coef.shape[1], lanes) * lanes
    block = lambda cols: pl.BlockSpec((1, rows, cols), lambda i: (i, 0, 0))
    return pl.pallas_call(
        product_kernel,
        grid=(n,),
        in_specs=[block(half), block(half), whole(*coef.shape)],
        out_specs=block(width),
        out_shape=jax.ShapeDtypeStruct((n, rows, width), jnp.bfloat16),
        compiler_params=pltpu.CompilerParams(vmem_limit_bytes=24 << 20),
        cost_estimate=pl.CostEstimate(
            flops=4 * n * rows * half * width, bytes_accessed=8 << 20, transcendentals=0
        ),
        name="product",
    )(held, traded, coef)


def shift(value, axis, step):
    n = lax.axis_size(axis)
    return lax.ppermute(value, axis, [(i, (i + step) % n) for i in range(n)])


def swap(value, axis):
    return lax.all_to_all(value, axis, 0, 0, tiled=True)


def gather(mine, axis):
    n = lax.axis_size(axis)
    return swap(jnp.broadcast_to(mine[None], (n,) + mine.shape), axis)


def shards(
    pair_integrals,
    occ_coef,
    vir_coef,
    metric_factor,
    block_rows,
    block_cols,
    block_count,
    occ_order,
):
    y, core = lax.axis_index("y"), lax.axis_index("c")
    nx, nz, ny = lax.axis_size("x"), lax.axis_size("z"), lax.axis_size("y")
    width = pair_integrals.shape[2]
    occ_width, ao_width = occ_coef.shape
    vir_width = vir_coef.shape[1]
    naux = nx * nz
    each = occ_width // naux
    place = jnp.stack([y, core]).astype(jnp.int32)

    own = pair_integrals[0]
    other = shift(own, "c", 1)
    order = occ_order.reshape(nx, nz, each).transpose(0, 2, 1).reshape(occ_width, 1)
    part = group_partial(
        own, other, occ_coef, order, block_rows, block_cols, block_count, place, nx, ny
    )
    vir_rows = lax.all_gather(vir_coef, "z", axis=0, tiled=True)
    share = swap(part.reshape((nx * ny,) + part.shape[2:]), ("x", "y")).reshape(part.shape)
    share = jnp.sum(share.astype(jnp.float32), 1).astype(jnp.bfloat16)
    held = gather(share.reshape(-1, share.shape[-1]), "y")
    held, vir_rows = lax.optimization_barrier((held, vir_rows))
    traded = shift(held, "c", 1)
    terms = swap(product(held, traded, halves(vir_rows, place), width), "x")
    pencil = jnp.sum(terms.astype(jnp.float32), 0).astype(jnp.bfloat16)
    pencil = pencil.reshape(nx, each, nz, -1, width).transpose(2, 0, 1, 3, 4)
    pencil = swap(pencil.reshape(nz, -1, width), "z")
    pencil = pencil.reshape(nz, nx, each, -1, width).transpose(2, 1, 0, 3, 4)
    pencil = pencil.reshape(each, naux, -1)[:, :, :vir_width]
    mixed = jnp.einsum("qp,kpv->qkv", metric_factor, pencil, preferred_element_type=jnp.float32)
    return mixed.astype(jnp.bfloat16)


def solution(mesh):
    aux, ao = mesh.devices.shape
    grid = Mesh(mesh.devices.reshape(4, aux // 4, ao // 2, 2), ("x", "z", "y", "c"))
    every = P()
    return jax.shard_map(
        shards,
        mesh=grid,
        in_specs=(P(("x", "z"), ("y", "c")), every, P(("x", "z"), ("y", "c"))) + (every,) * 5,
        out_specs=P(None, ("x", "z"), ("y", "c")),
        check_vma=False,
    )
```

time: 180 us -> 171 us (0.950)
  the two profiles are of different devices: /device:TPU:32 before, /device:TPU:48 now
where the time goes in v3:
time: 171 us
  blocking collectives  124 us (73%)
  between operations  13.5 us (8%)
  Pallas kernels  11.6 us (7%)
  waiting for transfers between devices  9.48 us (6%)
  local copies, waits for them, and re-layouts  5.95 us (3%)
  starting transfers between devices  3.95 us (2%)
    all_to_all x4, blocking collectives, swap(): return lax.all_to_all(value, axis, 0, 0, tiled=True)  124 us
    all_gather x1, waiting for transfers between devices, shards(): vir_rows = lax.all_gather(vir_coef, 'z', axis=0, tiled=True)  8.16 us
    pallas_call x1, Pallas kernels, group_partial(): pl.pallas_call(partial_kernel, grid_spec=pltpu.PrefetchScalarGridSpec(num...  6.76 us
    ppermute x2, starting transfers between devices, shift(): return lax.ppermute(value, axis, [(i, (i + step) % n) for i in range(n)])  3.95 us
    pallas_call x1, Pallas kernels, product(): pl.pallas_call(product_kernel, grid=(n,), in_specs=[block(half), block(ha...  3.74 us
  transfers between devices with their start and end apart: 3, of which 3 were waited for; matrix products, arithmetic and copies ran while one was open for 2% of the time, Pallas kernels for 5%

profile of v3, /device:TPU:48, one launch (start us, length us, event | category | flops | bytes accessed | tf_op | source)
XLA Modules:
  0.0 170.9 jit_solution(6107249371733737755)
XLA Ops:
  6.5 2.0 %collective-permute-start = (bf16[24,128,128]{2,1,0:T(8,128)(2,1)}, bf16[24,128,128]{2,1,0:T(8,128)(2,1)S(1)}, u32[]{:S(2)}, u32[]{:S(2)}) collective-permute-start(bf16[24,128,128]{2,1,0:T(8,128)(2,1)} %bitcast.23), channel_id=1, source_target_pairs={{0,1},{1,0},{2,3},{3,2},{4,5},{5,4},{6,7},{7,6},{8,9},{9,8},{10,11... | collective-permute-start | bytes 2359304 | tf_op jit(solution)/shard_map/ppermute | solution.py:144
  8.6 0.8 reshape.25
  9.5 0.8 reshape.34.order
  10.3 0.6 pad_add_fusion.place
  11.1 0.9 copy-done.3
  11.9 6.8 %group_partial.1 = bf16[4,4,80,768]{3,2,1,0:T(8,128)(2,1)} custom-call(s32[192]{0:T(256)} %rows.1, s32[192]{0:T(256)} %cols.1, s32[8]{0:T(128)} %counts.1, s32[2]{0:T(128)} %pad_add_fusion.place, bf16[24,128,128]{2,1,0:T(8,128)(2,1)} %bitcast.24, bf16[24,128,128]{2,1,0:T(8,128)(2,1)} %copy-done.3, bf16[320,6144]{1,0:T(8,128)(2,1)} %occ.1, ...), custom_call_target="tpu_custom_call" | custom-call | tf_op jit(solution)/shard_map/group_partial/pallas_call | solution.py:61
  18.7 33.2 %all_to_all.20 = bf16[16,80,768]{2,1,0:T(8,128)(2,1)S(1)} all-to-all(bf16[16,80,768]{2,1,0:T(8,128)(2,1)} %bitcast.18), channel_id=1, replica_groups=mesh['x'=4,'z'=16,'y'=4,'c'=2] {'x','y'}, dimensions={0} | all-to-all | bytes 3932160 | tf_op jit(solution)/shard_map/all_to_all | solution.py:148
  51.9 0.3 bitcast_reduce_fusion
  52.2 0.1 broadcast_in_dim.8
  52.3 26.5 %all_to_all.21.held = bf16[4,320,768]{2,1,0:T(8,128)(2,1)S(1)} all-to-all(bf16[4,320,768]{2,1,0:T(8,128)(2,1)S(1)} %broadcast_in_dim.8), channel_id=1, replica_groups=mesh['x'=4,'z'=16,'y'=4,'c'=2] {'y'}, dimensions={0} | all-to-all | bytes 3932160 | tf_op jit(solution)/shard_map/all_to_all | solution.py:148
  78.9 8.2 %all-gather.2.cloned.1.call-done.rows = bf16[1536,720]{1,0:T(8,128)(2,1)} async-done(((bf16[96,720]{1,0:T(8,128)(2,1)}), bf16[1536,720]{1,0:T(8,128)(2,1)}) %all-gather.2.cloned.1.call-update) | async-done | bytes 2211856 | tf_op jit(solution)/shard_map/all_gather | solution.py:181
  87.0 1.9 %collective-permute-start.1 = (bf16[4,320,768]{2,1,0:T(8,128)(2,1)S(1)}, bf16[4,320,768]{2,1,0:T(8,128)(2,1)S(1)}, u32[]{:S(2)}, u32[]{:S(2)}) collective-permute-start(bf16[4,320,768]{2,1,0:T(8,128)(2,1)S(1)} %all_to_all.21.held), channel_id=1, source_target_pairs={{0,1},{1,0},{2,3},{3,2},{4,5},{5,4},{6,7},{7,6},{8,9},{9,8},{10,11... | collective-permute-start | bytes 5898248 | tf_op jit(solution)/shard_map/ppermute | solution.py:144
  89.0 1.7 copy-done.1
  90.6 1.0 vir_halves.1.coef
  91.7 1.2 collective-permute-done.1.traded
  92.9 3.7 %product.1 = bf16[4,320,768]{2,1,0:T(8,128)(2,1)S(1)} custom-call(bf16[4,320,768]{2,1,0:T(8,128)(2,1)S(1)} %all_to_all.21.held, bf16[4,320,768]{2,1,0:T(8,128)(2,1)S(1)} %collective-permute-done.1.traded, bf16[1536,720]{1,0:T(8,128)(2,1)S(1)} %vir_halves.1.coef), custom_call_target="tpu_custom_call" | custom-call | flops 3019898880 | bytes 8388608 | tf_op jit(solution)/shard_map/product/pallas_call | solution.py:128
  96.6 29.7 %all_to_all.22 = bf16[4,320,768]{2,1,0:T(8,128)(2,1)S(1)} all-to-all(bf16[4,320,768]{2,1,0:T(8,128)(2,1)S(1)} %product.1), channel_id=1, replica_groups=mesh['x'=4,'z'=16,'y'=4,'c'=2] {'x'}, dimensions={0} | all-to-all | bytes 3932160 | tf_op jit(solution)/shard_map/all_to_all | solution.py:148
  126.3 0.6 reduce_sum.25
  126.9 0.6 reshape.29
  127.5 0.1 copy.16
  127.7 34.5 %all_to_all.23 = bf16[16,120,128]{2,1,0:T(8,128)(2,1)S(1)} all-to-all(bf16[16,120,128]{2,1,0:T(8,128)(2,1)S(1)} %copy.16), channel_id=1, replica_groups=mesh['x'=4,'z'=16,'y'=4,'c'=2] {'z'}, dimensions={0} | all-to-all | bytes 983040 | tf_op jit(solution)/shard_map/all_to_all | solution.py:148
  162.2 0.2 copy.18
  162.4 0.6 reshape.32
  163.0 1.1 fusion
  (12 shorter events, 0.4 us)
Async XLA Ops:
  6.5 156.5 %copy-start = (bf16[64,64]{1,0:T(8,128)(2,1)S(1)}, bf16[64,64]{1,0:T(8,128)(2,1)}, u32[]{:S(2)}) copy-start(bf16[64,64]{1,0:T(8,128)(2,1)} %param.11) | copy-start | bytes 24580
  6.5 80.5 %all-gather.2.cloned.1.call-start = ((), (), s32[]{:S(2)}) async-start(), calls=%async_computation.4 | async-start | bytes 2506752 | tf_op jit(solution)/shard_map/all_gather | solution.py:181
  6.5 4.5 %collective-permute-start = (bf16[24,128,128]{2,1,0:T(8,128)(2,1)}, bf16[24,128,128]{2,1,0:T(8,128)(2,1)S(1)}, u32[]{:S(2)}, u32[]{:S(2)}) collective-permute-start(bf16[24,128,128]{2,1,0:T(8,128)(2,1)} %bitcast.23), channel_id=1, source_target_pairs={{0,1},{1,0},{2,3},{3,2},{4,5},{5,4},{6,7},{7,6},{8,9},{9,8},{10,11... | collective-permute-start | bytes 2359304 | tf_op jit(solution)/shard_map/ppermute | solution.py:144
  11.1 0.9 copy-start.3
  52.3 36.6 %copy-start.2 = (s32[2]{0:T(128)S(1)}, s32[2]{0:T(128)}, u32[]{:S(2)}) copy-start(s32[2]{0:T(128)} %pad_add_fusion.place) | copy-start | bytes 28
  87.0 5.9 %collective-permute-start.1 = (bf16[4,320,768]{2,1,0:T(8,128)(2,1)S(1)}, bf16[4,320,768]{2,1,0:T(8,128)(2,1)S(1)}, u32[]{:S(2)}, u32[]{:S(2)}) collective-permute-start(bf16[4,320,768]{2,1,0:T(8,128)(2,1)S(1)} %all_to_all.21.held), channel_id=1, source_target_pairs={{0,1},{1,0},{2,3},{3,2},{4,5},{5,4},{6,7},{7,6},{8,9},{9,8},{10,11... | collective-permute-start | bytes 5898248 | tf_op jit(solution)/shard_map/ppermute | solution.py:144
  89.0 1.7 copy-start.1
Sparse Core Ops, SparseCore 0:
  9.4 77.5 all-gather.1

commit v4 on v3

--- a/solution.py
+++ b/solution.py
@@ -178,11 +178,19 @@
     part = group_partial(
         own, other, occ_coef, order, block_rows, block_cols, block_count, place, nx, ny
     )
+    part, vir_coef = lax.optimization_barrier((part, vir_coef))
     vir_rows = lax.all_gather(vir_coef, "z", axis=0, tiled=True)
-    share = swap(part.reshape((nx * ny,) + part.shape[2:]), ("x", "y")).reshape(part.shape)
-    share = jnp.sum(share.astype(jnp.float32), 1).astype(jnp.bfloat16)
+    def exchange(value):
+        terms = swap(value, ("x", "y")).reshape(part.shape)
+        return jnp.sum(terms.astype(jnp.float32), 1).astype(jnp.bfloat16)
+
+    share = lax.cond(
+        jnp.max(block_count) > 0,
+        exchange,
+        lambda value: jnp.zeros((nx,) + part.shape[2:], jnp.bfloat16),
+        part.reshape((nx * ny,) + part.shape[2:]),
+    )
     held = gather(share.reshape(-1, share.shape[-1]), "y")
-    held, vir_rows = lax.optimization_barrier((held, vir_rows))
     traded = shift(held, "c", 1)
     terms = swap(product(held, traded, halves(vir_rows, place), width), "x")
     pencil = jnp.sum(terms.astype(jnp.float32), 0).astype(jnp.bfloat16)

time: 171 us -> 165 us (0.965)
  the two profiles are of different devices: /device:TPU:48 before, /device:TPU:32 now
where the time goes in v4:
time: 165 us; the launch traced here: 164 us
  blocking collectives  110 us (67%)
  waiting for transfers between devices  14.6 us (9%)
  between operations  14.2 us (9%)
  Pallas kernels  11.9 us (7%)
  local copies, waits for them, and re-layouts  5.98 us (4%)
  starting transfers between devices  3.95 us (2%)
  other arithmetic  2.11 us (1%)
    all_to_all x4, blocking collectives, swap(): return lax.all_to_all(value, axis, 0, 0, tiled=True)  110 us
    all_gather x1, waiting for transfers between devices, shards(): vir_rows = lax.all_gather(vir_coef, 'z', axis=0, tiled=True)  14.5 us
    pallas_call x1, Pallas kernels, group_partial(): pl.pallas_call(partial_kernel, grid_spec=pltpu.PrefetchScalarGridSpec(num...  5.9 us
    pallas_call x1, Pallas kernels, product(): pl.pallas_call(product_kernel, grid=(n,), in_specs=[block(half), block(ha...  4.91 us
    ppermute x2, starting transfers between devices, shift(): return lax.ppermute(value, axis, [(i, (i + step) % n) for i in range(n)])  3.95 us
  transfers between devices with their start and end apart: 3, of which 2 were waited for; matrix products, arithmetic and copies ran while one was open for 2% of the time, Pallas kernels for 1%

profile of v4, /device:TPU:32, one launch (start us, length us, event | category | flops | bytes accessed | tf_op | source)
XLA Modules:
  0.0 164.2 jit_solution(3099631909844712824)
XLA Ops:
  6.5 2.0 %collective-permute-start = (bf16[24,128,128]{2,1,0:T(8,128)(2,1)}, bf16[24,128,128]{2,1,0:T(8,128)(2,1)S(1)}, u32[]{:S(2)}, u32[]{:S(2)}) collective-permute-start(bf16[24,128,128]{2,1,0:T(8,128)(2,1)} %bitcast.23), channel_id=1, source_target_pairs={{0,1},{1,0},{2,3},{3,2},{4,5},{5,4},{6,7},{7,6},{8,9},{9,8},{10,11... | collective-permute-start | bytes 2359304 | tf_op jit(solution)/shard_map/ppermute | solution.py:144
  8.6 0.8 reshape.28
  9.5 0.8 reshape.35.order
  10.3 0.6 pad_add_fusion.place
  11.1 0.9 copy-done.3
  11.9 5.9 %group_partial.1 = bf16[4,4,80,768]{3,2,1,0:T(8,128)(2,1)S(1)} custom-call(s32[192]{0:T(256)} %rows.1, s32[192]{0:T(256)} %cols.1, s32[8]{0:T(128)} %counts.1, s32[2]{0:T(128)} %pad_add_fusion.place, bf16[24,128,128]{2,1,0:T(8,128)(2,1)} %bitcast.24, bf16[24,128,128]{2,1,0:T(8,128)(2,1)} %copy-done.3, bf16[320,6144]{1,0:T(8,128)(2,1)} %occ.1, ...), custom_call_target="tpu_custom_call" | custom-call | tf_op jit(solution)/shard_map/group_partial/pallas_call | solution.py:61
  17.9 0.6 reduce_max.9
  19.2 34.8 %conditional.1 = (bf16[4,80,768]{2,1,0:T(8,128)(2,1)S(1)}) conditional(s32[]{:T(128)} %convert_element_type.13, () %tuple.12, bf16[4,4,80,768]{3,2,1,0:T(8,128)(2,1)S(1)} %group_partial.1), branch_computations={%region_1.0_spmd, %region_2.0_spmd} | conditional | flops 737280 | bytes 6389768 | solution.py:187
  19.2 34.5 %all_to_all.19 = bf16[16,80,768]{2,1,0:T(8,128)(2,1)S(1)} all-to-all(bf16[16,80,768]{2,1,0:T(8,128)(2,1)S(1)} %bitcast.18), channel_id=1, replica_groups=mesh['x'=4,'z'=16,'y'=4,'c'=2] {'x','y'}, dimensions={0} | all-to-all | bytes 3932160 | tf_op jit(solution)/shard_map/cond/branch_1_fun/all_to_all | solution.py:148
  53.7 0.3 bitcast_reduce_fusion
  53.9 0.1 broadcast_in_dim.8
  54.1 26.3 %all_to_all.20.held = bf16[4,320,768]{2,1,0:T(8,128)(2,1)S(1)} all-to-all(bf16[4,320,768]{2,1,0:T(8,128)(2,1)S(1)} %broadcast_in_dim.8), channel_id=1, replica_groups=mesh['x'=4,'z'=16,'y'=4,'c'=2] {'y'}, dimensions={0} | all-to-all | bytes 3932160 | tf_op jit(solution)/shard_map/all_to_all | solution.py:148
  80.4 1.9 %collective-permute-start.1 = (bf16[4,320,768]{2,1,0:T(8,128)(2,1)S(1)}, bf16[4,320,768]{2,1,0:T(8,128)(2,1)}, u32[]{:S(2)}, u32[]{:S(2)}) collective-permute-start(bf16[4,320,768]{2,1,0:T(8,128)(2,1)S(1)} %all_to_all.20.held), channel_id=1, source_target_pairs={{0,1},{1,0},{2,3},{3,2},{4,5},{5,4},{6,7},{7,6},{8,9},{9,8},{10,11... | collective-permute-start | bytes 5898248 | tf_op jit(solution)/shard_map/ppermute | solution.py:144
  82.3 14.5 %all-gather.2.cloned.1.call-done.rows = bf16[1536,720]{1,0:T(8,128)(2,1)} async-done(((bf16[96,720]{1,0:T(8,128)(2,1)}), bf16[1536,720]{1,0:T(8,128)(2,1)}) %all-gather.2.cloned.1.call-update) | async-done | bytes 2211856 | tf_op jit(solution)/shard_map/all_gather | solution.py:182
  96.9 1.7 %copy-done.1 = bf16[1536,720]{1,0:T(8,128)(2,1)S(1)} copy-done((bf16[1536,720]{1,0:T(8,128)(2,1)S(1)}, bf16[1536,720]{1,0:T(8,128)(2,1)}, u32[]{:S(2)}) %copy-start.1) | copy-done | bytes 2211864
  98.5 1.0 vir_halves.1.coef
  99.6 4.9 %product.1 = bf16[4,320,768]{2,1,0:T(8,128)(2,1)S(1)} custom-call(bf16[4,320,768]{2,1,0:T(8,128)(2,1)S(1)} %all_to_all.20.held, bf16[4,320,768]{2,1,0:T(8,128)(2,1)} %collective-permute-done.1.traded, bf16[1536,720]{1,0:T(8,128)(2,1)S(1)} %vir_halves.1.coef), custom_call_target="tpu_custom_call" | custom-call | flops 3019898880 | bytes 8388608 | tf_op jit(solution)/shard_map/product/pallas_call | solution.py:128
  104.5 20.5 %all_to_all.21 = bf16[4,320,768]{2,1,0:T(8,128)(2,1)S(1)} all-to-all(bf16[4,320,768]{2,1,0:T(8,128)(2,1)S(1)} %product.1), channel_id=1, replica_groups=mesh['x'=4,'z'=16,'y'=4,'c'=2] {'x'}, dimensions={0} | all-to-all | bytes 3932160 | tf_op jit(solution)/shard_map/all_to_all | solution.py:148
  125.0 0.6 reduce_sum.24
  125.5 0.6 reshape.30
  126.3 29.1 %all_to_all.22 = bf16[16,120,128]{2,1,0:T(8,128)(2,1)S(1)} all-to-all(bf16[16,120,128]{2,1,0:T(8,128)(2,1)S(1)} %copy.16), channel_id=1, replica_groups=mesh['x'=4,'z'=16,'y'=4,'c'=2] {'z'}, dimensions={0} | all-to-all | bytes 983040 | tf_op jit(solution)/shard_map/all_to_all | solution.py:148
  155.5 0.2 copy.18
  155.7 0.6 reshape.33
  156.3 1.1 fusion
  (16 shorter events, 0.5 us)
Async XLA Ops:
  6.5 149.7 %copy-start = (bf16[64,64]{1,0:T(8,128)(2,1)S(1)}, bf16[64,64]{1,0:T(8,128)(2,1)}, u32[]{:S(2)}) copy-start(bf16[64,64]{1,0:T(8,128)(2,1)} %param.13) | copy-start | bytes 24580
  6.5 90.3 %all-gather.2.cloned.1.call-start = ((), (), s32[]{:S(2)}) async-start(), calls=%async_computation.4 | async-start | bytes 2506752 | tf_op jit(solution)/shard_map/all_gather | solution.py:182
  6.5 4.5 %collective-permute-start = (bf16[24,128,128]{2,1,0:T(8,128)(2,1)}, bf16[24,128,128]{2,1,0:T(8,128)(2,1)S(1)}, u32[]{:S(2)}, u32[]{:S(2)}) collective-permute-start(bf16[24,128,128]{2,1,0:T(8,128)(2,1)} %bitcast.23), channel_id=1, source_target_pairs={{0,1},{1,0},{2,3},{3,2},{4,5},{5,4},{6,7},{7,6},{8,9},{9,8},{10,11... | collective-permute-start | bytes 2359304 | tf_op jit(solution)/shard_map/ppermute | solution.py:144
  11.0 6.9 %copy-start.4 = (s32[8]{0:T(128)S(1)}, s32[8]{0:T(128)}, u32[]{:S(2)}) copy-start(s32[8]{0:T(128)} %counts.1) | copy-start | bytes 100
  11.1 0.9 copy-start.3
  54.1 42.8 %copy-start.2 = (s32[2]{0:T(128)S(1)}, s32[2]{0:T(128)}, u32[]{:S(2)}) copy-start(s32[2]{0:T(128)} %pad_add_fusion.place) | copy-start | bytes 28
  80.4 19.2 %collective-permute-start.1 = (bf16[4,320,768]{2,1,0:T(8,128)(2,1)S(1)}, bf16[4,320,768]{2,1,0:T(8,128)(2,1)}, u32[]{:S(2)}, u32[]{:S(2)}) collective-permute-start(bf16[4,320,768]{2,1,0:T(8,128)(2,1)S(1)} %all_to_all.20.held), channel_id=1, source_target_pairs={{0,1},{1,0},{2,3},{3,2},{4,5},{5,4},{6,7},{7,6},{8,9},{9,8},{10,11... | collective-permute-start | bytes 5898248 | tf_op jit(solution)/shard_map/ppermute | solution.py:144
  96.9 1.7 %copy-start.1 = (bf16[1536,720]{1,0:T(8,128)(2,1)S(1)}, bf16[1536,720]{1,0:T(8,128)(2,1)}, u32[]{:S(2)}) copy-start(bf16[1536,720]{1,0:T(8,128)(2,1)} %all-gather.2.cloned.1.call-done.rows) | copy-start | bytes 6635524
Sparse Core Ops, SparseCore 0:
  18.0 78.8 all-gather.1

commit v5 on v4

--- a/solution.py
+++ b/solution.py
@@ -17,11 +17,12 @@
     y, core = place[0], place[1]
     pick = lax.broadcasted_iota(jnp.int32, (occ_width, occ_width), 1) == order[...]
     pick = jnp.where(pick, 1.0, 0.0).astype(jnp.bfloat16)
-    for row in range(coef.shape[0]):
+    for row in range(0, coef.shape[0], 2):
         chosen = jnp.dot(
-            pick, occ[:, row * width : (row + 1) * width], preferred_element_type=jnp.float32
-        )
-        coef[row] = chosen.astype(coef.dtype)
+            pick, occ[:, row * width : (row + 2) * width], preferred_element_type=jnp.float32
+        ).astype(coef.dtype)
+        coef[row] = chosen[:, :width]
+        coef[row + 1] = chosen[:, width:]
     total[...] = jnp.zeros_like(total)
 
     for which, blocks in ((core, own), (1 - core, other)):
@@ -113,21 +114,22 @@
 
 
 def product_kernel(held, traded, coef, out):
-    half, cut = held.shape[2], coef.shape[1]
-    total = jnp.dot(held[0], coef[:half], preferred_element_type=jnp.float32)
-    total += jnp.dot(traded[0], coef[half:], preferred_element_type=jnp.float32)
-    out[0, :, :cut] = total.astype(out.dtype)
+    (many, rows, half), cut = held.shape, coef.shape[1]
+    flat = lambda ref: ref[...].reshape(many * rows, half)
+    total = jnp.dot(flat(held), coef[:half], preferred_element_type=jnp.float32)
+    total += jnp.dot(flat(traded), coef[half:], preferred_element_type=jnp.float32)
+    out[:, :, :cut] = total.astype(out.dtype).reshape(many, rows, cut)
     if cut < out.shape[2]:
-        out[0, :, cut:] = jnp.zeros((total.shape[0], out.shape[2] - cut), out.dtype)
+        out[:, :, cut:] = jnp.zeros((many, rows, out.shape[2] - cut), out.dtype)
 
 
 def product(held, traded, coef, lanes):
     n, rows, half = held.shape
     width = pl.cdiv(coef.shape[1], lanes) * lanes
-    block = lambda cols: pl.BlockSpec((1, rows, cols), lambda i: (i, 0, 0))
+    block = lambda cols: pl.BlockSpec((2, rows, cols), lambda i: (i, 0, 0))
     return pl.pallas_call(
         product_kernel,
-        grid=(n,),
+        grid=(n // 2,),
         in_specs=[block(half), block(half), whole(*coef.shape)],
         out_specs=block(width),
         out_shape=jax.ShapeDtypeStruct((n, rows, width), jnp.bfloat16),

time: 165 us -> 165 us (level)
  blocking collectives: 110 us -> 112 us
where the time goes in v5:
time: 165 us; the launch traced here: 164 us
  blocking collectives  112 us (68%)
  waiting for transfers between devices  14.6 us (9%)
  between operations  14.2 us (9%)
  Pallas kernels  10.7 us (6%)
  local copies, waits for them, and re-layouts  5.98 us (4%)
  starting transfers between devices  3.95 us (2%)
  other arithmetic  2.11 us (1%)
    all_to_all x4, blocking collectives, swap(): return lax.all_to_all(value, axis, 0, 0, tiled=True)  112 us
    all_gather x1, waiting for transfers between devices, shards(): vir_rows = lax.all_gather(vir_coef, 'z', axis=0, tiled=True)  14.4 us
    pallas_call x1, Pallas kernels, group_partial(): pl.pallas_call(partial_kernel, grid_spec=pltpu.PrefetchScalarGridSpec(num...  5.07 us
    pallas_call x1, Pallas kernels, product(): pl.pallas_call(product_kernel, grid=(n // 2,), in_specs=[block(half), blo...  4.62 us
    ppermute x2, starting transfers between devices, shift(): return lax.ppermute(value, axis, [(i, (i + step) % n) for i in range(n)])  3.95 us
  transfers between devices with their start and end apart: 3, of which 2 were waited for; matrix products, arithmetic and copies ran while one was open for 2% of the time, Pallas kernels for 1%

profile of v5, /device:TPU:32, one launch (start us, length us, event | category | flops | bytes accessed | tf_op | source)
XLA Modules:
  0.0 164.4 jit_solution(17105443235929041571)
XLA Ops:
  6.5 2.0 %collective-permute-start = (bf16[24,128,128]{2,1,0:T(8,128)(2,1)}, bf16[24,128,128]{2,1,0:T(8,128)(2,1)S(1)}, u32[]{:S(2)}, u32[]{:S(2)}) collective-permute-start(bf16[24,128,128]{2,1,0:T(8,128)(2,1)} %bitcast.23), channel_id=1, source_target_pairs={{0,1},{1,0},{2,3},{3,2},{4,5},{5,4},{6,7},{7,6},{8,9},{9,8},{10,11... | collective-permute-start | bytes 2359304 | tf_op jit(solution)/shard_map/ppermute | solution.py:146
  8.6 0.8 reshape.28
  9.5 0.8 reshape.35.order
  10.3 0.6 pad_add_fusion.place
  11.1 0.9 copy-done.3
  11.9 5.1 %group_partial.1 = bf16[4,4,80,768]{3,2,1,0:T(8,128)(2,1)S(1)} custom-call(s32[192]{0:T(256)} %rows.1, s32[192]{0:T(256)} %cols.1, s32[8]{0:T(128)} %counts.1, s32[2]{0:T(128)} %pad_add_fusion.place, bf16[24,128,128]{2,1,0:T(8,128)(2,1)} %bitcast.24, bf16[24,128,128]{2,1,0:T(8,128)(2,1)} %copy-done.3, bf16[320,6144]{1,0:T(8,128)(2,1)} %occ.1, ...), custom_call_target="tpu_custom_call" | custom-call | tf_op jit(solution)/shard_map/group_partial/pallas_call | solution.py:62
  17.1 0.6 reduce_max.9
  18.3 36.3 %conditional.1 = (bf16[4,80,768]{2,1,0:T(8,128)(2,1)S(1)}) conditional(s32[]{:T(128)} %convert_element_type.13, () %tuple.12, bf16[4,4,80,768]{3,2,1,0:T(8,128)(2,1)S(1)} %group_partial.1), branch_computations={%region_1.0_spmd, %region_2.0_spmd} | conditional | flops 737280 | bytes 6389768 | solution.py:189
  18.4 36.0 %all_to_all.19 = bf16[16,80,768]{2,1,0:T(8,128)(2,1)S(1)} all-to-all(bf16[16,80,768]{2,1,0:T(8,128)(2,1)S(1)} %bitcast.18), channel_id=1, replica_groups=mesh['x'=4,'z'=16,'y'=4,'c'=2] {'x','y'}, dimensions={0} | all-to-all | bytes 3932160 | tf_op jit(solution)/shard_map/cond/branch_1_fun/all_to_all | solution.py:150
  54.4 0.3 bitcast_reduce_fusion
  54.8 26.4 %all_to_all.20.held = bf16[4,320,768]{2,1,0:T(8,128)(2,1)S(1)} all-to-all(bf16[4,320,768]{2,1,0:T(8,128)(2,1)S(1)} %broadcast_in_dim.8), channel_id=1, replica_groups=mesh['x'=4,'z'=16,'y'=4,'c'=2] {'y'}, dimensions={0} | all-to-all | bytes 3932160 | tf_op jit(solution)/shard_map/all_to_all | solution.py:150
  81.2 1.9 %collective-permute-start.1 = (bf16[4,320,768]{2,1,0:T(8,128)(2,1)S(1)}, bf16[4,320,768]{2,1,0:T(8,128)(2,1)}, u32[]{:S(2)}, u32[]{:S(2)}) collective-permute-start(bf16[4,320,768]{2,1,0:T(8,128)(2,1)S(1)} %all_to_all.20.held), channel_id=1, source_target_pairs={{0,1},{1,0},{2,3},{3,2},{4,5},{5,4},{6,7},{7,6},{8,9},{9,8},{10,11... | collective-permute-start | bytes 5898248 | tf_op jit(solution)/shard_map/ppermute | solution.py:146
  83.1 14.4 %all-gather.2.cloned.1.call-done.rows = bf16[1536,720]{1,0:T(8,128)(2,1)} async-done(((bf16[96,720]{1,0:T(8,128)(2,1)}), bf16[1536,720]{1,0:T(8,128)(2,1)}) %all-gather.2.cloned.1.call-update) | async-done | bytes 2211856 | tf_op jit(solution)/shard_map/all_gather | solution.py:184
  97.5 1.7 %copy-done.1 = bf16[1536,720]{1,0:T(8,128)(2,1)S(1)} copy-done((bf16[1536,720]{1,0:T(8,128)(2,1)S(1)}, bf16[1536,720]{1,0:T(8,128)(2,1)}, u32[]{:S(2)}) %copy-start.1) | copy-done | bytes 2211864
  99.2 1.0 vir_halves.1.coef
  100.3 4.6 %product.1 = bf16[4,320,768]{2,1,0:T(8,128)(2,1)S(1)} custom-call(bf16[4,320,768]{2,1,0:T(8,128)(2,1)S(1)} %all_to_all.20.held, bf16[4,320,768]{2,1,0:T(8,128)(2,1)} %collective-permute-done.1.traded, bf16[1536,720]{1,0:T(8,128)(2,1)S(1)} %vir_halves.1.coef), custom_call_target="tpu_custom_call" | custom-call | flops 3019898880 | bytes 8388608 | tf_op jit(solution)/shard_map/product/pallas_call | solution.py:130
  104.9 20.0 %all_to_all.21 = bf16[4,320,768]{2,1,0:T(8,128)(2,1)S(1)} all-to-all(bf16[4,320,768]{2,1,0:T(8,128)(2,1)S(1)} %product.1), channel_id=1, replica_groups=mesh['x'=4,'z'=16,'y'=4,'c'=2] {'x'}, dimensions={0} | all-to-all | bytes 3932160 | tf_op jit(solution)/shard_map/all_to_all | solution.py:150
  124.9 0.6 reduce_sum.24
  125.5 0.6 reshape.30
  126.1 0.1 copy.16
  126.2 29.4 %all_to_all.22 = bf16[16,120,128]{2,1,0:T(8,128)(2,1)S(1)} all-to-all(bf16[16,120,128]{2,1,0:T(8,128)(2,1)S(1)} %copy.16), channel_id=1, replica_groups=mesh['x'=4,'z'=16,'y'=4,'c'=2] {'z'}, dimensions={0} | all-to-all | bytes 983040 | tf_op jit(solution)/shard_map/all_to_all | solution.py:150
  155.7 0.2 copy.18
  155.9 0.6 reshape.33
  156.5 1.1 fusion
  (16 shorter events, 0.5 us)
Async XLA Ops:
  6.5 149.9 %copy-start = (bf16[64,64]{1,0:T(8,128)(2,1)S(1)}, bf16[64,64]{1,0:T(8,128)(2,1)}, u32[]{:S(2)}) copy-start(bf16[64,64]{1,0:T(8,128)(2,1)} %param.13) | copy-start | bytes 24580
  6.5 91.0 %all-gather.2.cloned.1.call-start = ((), (), s32[]{:S(2)}) async-start(), calls=%async_computation.4 | async-start | bytes 2506752 | tf_op jit(solution)/shard_map/all_gather | solution.py:184
  6.5 4.5 %collective-permute-start = (bf16[24,128,128]{2,1,0:T(8,128)(2,1)}, bf16[24,128,128]{2,1,0:T(8,128)(2,1)S(1)}, u32[]{:S(2)}, u32[]{:S(2)}) collective-permute-start(bf16[24,128,128]{2,1,0:T(8,128)(2,1)} %bitcast.23), channel_id=1, source_target_pairs={{0,1},{1,0},{2,3},{3,2},{4,5},{5,4},{6,7},{7,6},{8,9},{9,8},{10,11... | collective-permute-start | bytes 2359304 | tf_op jit(solution)/shard_map/ppermute | solution.py:146
  11.0 6.1 %copy-start.4 = (s32[8]{0:T(128)S(1)}, s32[8]{0:T(128)}, u32[]{:S(2)}) copy-start(s32[8]{0:T(128)} %counts.1) | copy-start | bytes 100
  11.1 0.9 copy-start.3
  54.8 42.7 %copy-start.2 = (s32[2]{0:T(128)S(1)}, s32[2]{0:T(128)}, u32[]{:S(2)}) copy-start(s32[2]{0:T(128)} %pad_add_fusion.place) | copy-start | bytes 28
  81.2 19.1 %collective-permute-start.1 = (bf16[4,320,768]{2,1,0:T(8,128)(2,1)S(1)}, bf16[4,320,768]{2,1,0:T(8,128)(2,1)}, u32[]{:S(2)}, u32[]{:S(2)}) collective-permute-start(bf16[4,320,768]{2,1,0:T(8,128)(2,1)S(1)} %all_to_all.20.held), channel_id=1, source_target_pairs={{0,1},{1,0},{2,3},{3,2},{4,5},{5,4},{6,7},{7,6},{8,9},{9,8},{10,11... | collective-permute-start | bytes 5898248 | tf_op jit(solution)/shard_map/ppermute | solution.py:146
  97.5 1.7 %copy-start.1 = (bf16[1536,720]{1,0:T(8,128)(2,1)S(1)}, bf16[1536,720]{1,0:T(8,128)(2,1)}, u32[]{:S(2)}) copy-start(bf16[1536,720]{1,0:T(8,128)(2,1)} %all-gather.2.cloned.1.call-done.rows) | copy-start | bytes 6635524
Sparse Core Ops, SparseCore 0:
  17.2 80.3 all-gather.1
